TPU v7x, 512 devices: a whole 4x8x8 slice. The times are simulated.
512 devices in a mesh: dp: 4 (over x), expert: 128 (over y, z, core).
Axes of the slice: x: 4, y: 8, z: 8, core: 2. Of those that a mesh axis runs over, the one named last changes fastest.
Arguments:
- out_grad: bfloat16 [8192, 1536], P(('dp', 'expert')), may hold values from -1.5 to 1.5
- routes: int32 [8192, 8], P(('dp', 'expert')), may hold values from 0 to 127, all different within a row; in each aligned block of 16 rows (0 to 15, 16 to 31, ...) at most 2 rows name the same one
- gate_probs: float32 [8192, 8], P(('dp', 'expert')), may hold values from 0.05 to 1
- saved_inputs: bfloat16 [4, 128, 256, 1536], P('dp', 'expert'), may hold values from -6 to 6
- w_gate: bfloat16 [128, 1536, 384], P('expert', 'dp'), may hold values from -0.15625 to 0.15625
- w_up: bfloat16 [128, 1536, 384], P('expert', 'dp'), may hold values from -0.15625 to 0.15625
- w_down: bfloat16 [128, 1536, 384], P('expert', 'dp'), may hold values from -0.3125 to 0.3125
Outputs:
- token_grad: bfloat16 [8192, 1536], P(('dp', 'expert'))
- prob_grad: float32 [8192, 8], P(('dp', 'expert'))
- grad_gate: bfloat16 [128, 1536, 384], P('expert', 'dp')
- grad_up: bfloat16 [128, 1536, 384], P('expert', 'dp')
- grad_down: bfloat16 [128, 1536, 384], P('expert', 'dp')
Inputs may be any that keep to these rules, and one draw needn't show every extreme that they name: `routes`: within the tokens of one device no expert is named by more than 2 entries, a bound that some block reaches; a token names 8 different experts.
All inputs are finite; a program needn't handle non-finite values.
Results may differ from a plain program's by a relative error of at most 0.02.
Values may be sent and summed in bfloat16 or wider, within the bound.
No kernel may reach another device: no remote copies, remote signals or barrier semaphores. Data moves between devices by JAX's collectives and lax.ppermute only.
A program may use at most 64 MiB of HBM per device.

v0:
```python
import jax
import jax.numpy as jnp
from jax import lax
from jax.sharding import PartitionSpec as P

TOP = 8


def expert_rows(inputs_rows, grad_rows, prob, gate_w, up_w, down_w):
    pre_gate = jnp.dot(inputs_rows, gate_w, preferred_element_type=jnp.float32)
    pre_up = jnp.dot(inputs_rows, up_w, preferred_element_type=jnp.float32)
    sigma_g = jax.nn.sigmoid(pre_gate)
    activated = pre_gate * sigma_g
    hidden = activated * pre_up
    dh_raw = jnp.dot(grad_rows, down_w, preferred_element_type=jnp.float32)
    row_prob = jnp.sum(hidden * dh_raw, axis=1)
    scaled_hidden = (prob[:, None] * hidden).astype(jnp.bfloat16)
    dh_full = prob[:, None] * dh_raw
    d_up = (dh_full * activated).astype(jnp.bfloat16)
    d_gate = (dh_full * pre_up * sigma_g * (1.0 + pre_gate * (1.0 - sigma_g))).astype(jnp.bfloat16)
    row_grad = (
        jnp.dot(d_gate, gate_w.T, preferred_element_type=jnp.float32)
        + jnp.dot(d_up, up_w.T, preferred_element_type=jnp.float32)
    ).astype(jnp.bfloat16)
    return (row_grad, row_prob, d_gate, d_up, scaled_hidden)


def shards(out_grad, routes, gate_probs, saved_inputs, w_gate, w_up, w_down):
    tok_rows = out_grad.shape[0]
    width = out_grad.shape[1]
    experts_here = lax.axis_size("expert")
    capacity = saved_inputs.shape[2] // experts_here
    all_slots = saved_inputs.shape[2]
    flat_routes = routes.reshape(-1)
    onehot = (flat_routes[:, None] == jnp.arange(experts_here, dtype=jnp.int32)[None, :]).astype(
        jnp.int32
    )
    running = jnp.cumsum(onehot, axis=0)
    slot_of = jnp.sum(onehot * (running - 1), axis=1)
    target = flat_routes * capacity + slot_of
    repeated = jnp.repeat(out_grad, TOP, axis=0)
    send_rows = jnp.zeros((all_slots, width), jnp.bfloat16).at[target].set(repeated)
    send_prob = jnp.zeros((all_slots,), jnp.float32).at[target].set(gate_probs.reshape(-1))
    send_rows = send_rows.reshape(experts_here, capacity, width)
    send_prob = send_prob.reshape(experts_here, capacity)
    recv_rows, recv_prob = (
        lax.all_to_all(send_rows, "expert", split_axis=0, concat_axis=0, tiled=True),
        lax.all_to_all(
            send_prob.astype(jnp.bfloat16), "expert", split_axis=0, concat_axis=0, tiled=True
        ).astype(send_prob.dtype),
    )
    gathered = (
        lax.all_gather(w_gate, "dp", axis=1, tiled=True),
        lax.all_gather(w_up, "dp", axis=1, tiled=True),
        lax.all_gather(w_down, "dp", axis=1, tiled=True),
    )
    gate_w = gathered[0][0]
    up_w = gathered[1][0]
    down_w = gathered[2][0]
    inputs_rows = saved_inputs[0, 0]
    grad_rows = recv_rows.reshape(all_slots, width)
    prob_rows = recv_prob.reshape(all_slots)
    row_grad, row_prob, d_gate, d_up, scaled_hidden = expert_rows(
        inputs_rows, grad_rows, prob_rows, gate_w, up_w, down_w
    )
    part_gate = jnp.dot(inputs_rows.T, d_gate, preferred_element_type=jnp.float32)
    part_up = jnp.dot(inputs_rows.T, d_up, preferred_element_type=jnp.float32)
    part_down = jnp.dot(grad_rows.T, scaled_hidden, preferred_element_type=jnp.float32)
    back_rows, back_prob = (
        lax.all_to_all(
            row_grad.reshape(experts_here, capacity, width),
            "expert",
            split_axis=0,
            concat_axis=0,
            tiled=True,
        ),
        lax.all_to_all(
            row_prob.reshape(experts_here, capacity).astype(jnp.bfloat16),
            "expert",
            split_axis=0,
            concat_axis=0,
            tiled=True,
        ).astype(jnp.float32),
    )
    pair_rows = back_rows.reshape(all_slots, width)[target]
    token_grad = jnp.sum(
        pair_rows.reshape(tok_rows, TOP, width).astype(jnp.float32), axis=1
    ).astype(jnp.bfloat16)
    prob_grad = back_prob.reshape(all_slots)[target].reshape(tok_rows, TOP)
    summed = (
        lax.psum_scatter(
            part_gate[None].astype(jnp.bfloat16), "dp", scatter_dimension=1, tiled=True
        ).astype(jnp.float32),
        lax.psum_scatter(
            part_up[None].astype(jnp.bfloat16), "dp", scatter_dimension=1, tiled=True
        ).astype(jnp.float32),
        lax.psum_scatter(
            part_down[None].astype(jnp.bfloat16), "dp", scatter_dimension=1, tiled=True
        ).astype(jnp.float32),
    )
    grad_gate = summed[0].astype(jnp.bfloat16)
    grad_up = summed[1].astype(jnp.bfloat16)
    grad_down = summed[2].astype(jnp.bfloat16)
    return (token_grad, prob_grad, grad_gate, grad_up, grad_down)


def solution(mesh):
    return jax.shard_map(
        shards,
        mesh=mesh,
        in_specs=(
            P(("dp", "expert"), None),
            P(("dp", "expert"), None),
            P(("dp", "expert"), None),
            P("dp", "expert", None, None),
            P("expert", "dp", None),
            P("expert", "dp", None),
            P("expert", "dp", None),
        ),
        out_specs=(
            P(("dp", "expert"), None),
            P(("dp", "expert"), None),
            P("expert", "dp", None),
            P("expert", "dp", None),
            P("expert", "dp", None),
        ),
        check_vma=False,
    )
```

profile of v0, /device:TPU:1, one launch (start us, length us, event | category | flops | bytes accessed | tf_op | source)
XLA Modules:
  0.0 221.7 jit_solution(12283877655016537545)
XLA Ops:
  13.5 18.4 %all-to-all-start = ((bf16[128,1,2]{2,1,0:T(2,128)(2,1)}), bf16[128,1,2]{2,1,0:T(2,128)(2,1)S(1)}, u32[]{:S(2)}, u32[]{:S(2)}) async-start(bf16[128,1,2]{2,1,0:T(2,128)(2,1)} %convert_element_type.113), calls=%async_computation | async-start | bytes 131072 | tf_op jit(solution)/shard_map/all_to_all | solution.py:48
  31.9 1.7 scatter_custom_fusion.1
  34.8 8.5 %all-to-all-done = bf16[128,1,2]{2,1,0:T(2,128)(2,1)S(1)} async-done(((bf16[128,1,2]{2,1,0:T(2,128)(2,1)}), bf16[128,1,2]{2,1,0:T(2,128)(2,1)S(1)}, u32[]{:S(2)}, u32[]{:S(2)}) %all-to-all-start) | async-done | bytes 544 | tf_op jit(solution)/shard_map/all_to_all | solution.py:48
  43.4 5.7 %all-to-all-start.1 = ((bf16[128,2,1536]{2,1,0:T(2,128)(2,1)}), bf16[128,2,1536]{2,1,0:T(2,128)(2,1)S(1)}, u32[]{:S(2)}, u32[]{:S(2)}) async-start(bf16[128,2,1536]{2,1,0:T(2,128)(2,1)} %reshape.108), calls=%async_computation.1 | async-start | bytes 1572864 | tf_op jit(solution)/shard_map/all_to_all | solution.py:47
  50.2 24.0 %all-to-all-done.1 = bf16[128,2,1536]{2,1,0:T(2,128)(2,1)S(1)} async-done(((bf16[128,2,1536]{2,1,0:T(2,128)(2,1)}), bf16[128,2,1536]{2,1,0:T(2,128)(2,1)S(1)}, u32[]{:S(2)}, u32[]{:S(2)}) %all-to-all-start.1) | async-done | bytes 786464 | tf_op jit(solution)/shard_map/all_to_all | solution.py:47
  74.5 2.1 fusion.6
  76.9 1.8 fusion.9
  78.7 30.6 %all-gather.4.cloned.1.call-done = bf16[1,1536,384]{2,1,0:T(8,128)(2,1)} async-done(((bf16[1,384,384]{2,1,0:T(8,128)(2,1)}), bf16[1,1536,384]{2,1,0:T(8,128)(2,1)}) %all-gather.4.cloned.1.call-update) | async-done | bytes 1179664 | tf_op jit(solution)/shard_map/all_gather | solution.py:55
  109.4 2.0 multiply_reduce_fusion
  111.4 1.5 fusion.1
  113.0 6.3 %copy.32 = bf16[1,1536,384]{2,0,1:T(2,128)(2,1)S(1)} copy(bf16[1,1536,384]{1,2,0:T(8,128)(2,1)} %fusion.1) | data formatting | bytes 2359296
  119.2 1.2 copy.43
  120.5 1.5 fusion.2
  122.0 6.3 %copy.34 = bf16[1,1536,384]{2,0,1:T(2,128)(2,1)S(1)} copy(bf16[1,1536,384]{1,2,0:T(8,128)(2,1)} %fusion.2) | data formatting | bytes 2359296
  130.4 15.2 %all-to-all-start.3 = ((bf16[128,1,2]{2,1,0:T(2,128)(2,1)}), bf16[128,1,2]{2,1,0:T(2,128)(2,1)S(1)}, u32[]{:S(2)}, u32[]{:S(2)}) async-start(bf16[128,1,2]{2,1,0:T(2,128)(2,1)} %convert_element_type.114), calls=%async_computation.3 | async-start | bytes 131072 | tf_op jit(solution)/shard_map/all_to_all | solution.py:77
  145.7 2.7 %fusion.3 = bf16[1,1536,384]{2,1,0:T(8,128)(2,1)} fusion(bf16[256,1536]{1,0:T(8,128)(2,1)S(1)} %copy-done.4, f32[256]{0:T(256)S(1)} %reshape.114, f32[256,384]{1,0:T(8,128)} %copy-done.7, f32[256,384]{1,0:T(8,128)S(1)} %copy-done.6), kind=kOutput, calls=%fused_computation.11 | convolution fusion | flops 303267840 | bytes 2753536 | tf_op jit(solution)/shard_map/dot_general | solution.py:68
  148.4 1.2 copy-done.2
  152.8 4.3 %all-to-all-done.3 = bf16[128,1,2]{2,1,0:T(2,128)(2,1)S(1)} async-done(((bf16[128,1,2]{2,1,0:T(2,128)(2,1)}), bf16[128,1,2]{2,1,0:T(2,128)(2,1)S(1)}, u32[]{:S(2)}, u32[]{:S(2)}) %all-to-all-start.3) | async-done | bytes 544 | tf_op jit(solution)/shard_map/all_to_all | solution.py:77
  157.1 9.4 %all-to-all-start.2 = ((bf16[128,2,1536]{2,1,0:T(2,128)(2,1)}), bf16[128,2,1536]{2,1,0:T(2,128)(2,1)S(1)}, u32[]{:S(2)}, u32[]{:S(2)}) async-start(bf16[128,2,1536]{2,1,0:T(2,128)(2,1)} %reshape.110), calls=%async_computation.2 | async-start | bytes 1572864 | tf_op jit(solution)/shard_map/all_to_all | solution.py:70
  166.9 1.3 gather_fusion.1
  168.9 22.8 %all-to-all-done.2 = bf16[128,2,1536]{2,1,0:T(2,128)(2,1)S(1)} async-done(((bf16[128,2,1536]{2,1,0:T(2,128)(2,1)}), bf16[128,2,1536]{2,1,0:T(2,128)(2,1)S(1)}, u32[]{:S(2)}, u32[]{:S(2)}) %all-to-all-start.2) | async-done | bytes 786464 | tf_op jit(solution)/shard_map/all_to_all | solution.py:70
  193.7 1.3 reshape_bitcast_fusion.1
  195.8 1.3 reshape_bitcast_fusion
  197.8 17.1 %reduce-scatter.8.cloned.1.call-done = bf16[1,384,384]{2,1,0:T(8,128)(2,1)} async-done(((bf16[1,1536,384]{2,1,0:T(8,128)(2,1)}), bf16[1,384,384]{2,1,0:T(8,128)(2,1)}) %reduce-scatter.8.cloned.1.call-update) | async-done | bytes 294928 | tf_op jit(solution)/shard_map/reduce_scatter | solution.py:97
  (64 shorter events, 19.0 us)
Async XLA Ops:
  7.2 67.4 %copy-start = (bf16[1,1,256,1536]{3,2,1,0:T(8,128)(2,1)S(1)}, bf16[1,1,256,1536]{3,2,1,0:T(8,128)(2,1)}, u32[]{:S(2)}) copy-start(bf16[1,1,256,1536]{3,2,1,0:T(8,128)(2,1)} %param.10) | copy-start | bytes 2359300
  7.2 67.3 %all-gather.8.cloned.1.call-start = ((), (), s32[]{:S(2)}) async-start(), calls=%async_computation.9 | async-start | bytes 1474560 | tf_op jit(solution)/shard_map/all_gather | solution.py:53
  7.9 69.0 %all-gather.6.cloned.1.call-start = ((), (), s32[]{:S(2)}) async-start(), calls=%async_computation.8 | async-start | bytes 1474560 | tf_op jit(solution)/shard_map/all_gather | solution.py:54
  13.5 29.9 %all-to-all-start = ((bf16[128,1,2]{2,1,0:T(2,128)(2,1)}), bf16[128,1,2]{2,1,0:T(2,128)(2,1)S(1)}, u32[]{:S(2)}, u32[]{:S(2)}) async-start(bf16[128,1,2]{2,1,0:T(2,128)(2,1)} %convert_element_type.113), calls=%async_computation | async-start | bytes 131072 | tf_op jit(solution)/shard_map/all_to_all | solution.py:48
  43.4 30.8 %all-to-all-start.1 = ((bf16[128,2,1536]{2,1,0:T(2,128)(2,1)}), bf16[128,2,1536]{2,1,0:T(2,128)(2,1)S(1)}, u32[]{:S(2)}, u32[]{:S(2)}) async-start(bf16[128,2,1536]{2,1,0:T(2,128)(2,1)} %reshape.108), calls=%async_computation.1 | async-start | bytes 1572864 | tf_op jit(solution)/shard_map/all_to_all | solution.py:47
  49.1 60.3 %all-gather.4.cloned.1.call-start = ((), (), s32[]{:S(2)}) async-start(), calls=%async_computation.7 | async-start | bytes 1474560 | tf_op jit(solution)/shard_map/all_gather | solution.py:55
  49.8 143.9 %reduce-scatter.10.cloned.1.call-start = ((), (), s32[]{:S(2)}) async-start(), calls=%async_computation.11 | async-start | bytes 1474560
  74.5 34.9 %copy-start.3 = (bf16[256,1536]{1,0:T(8,128)(2,1)}, bf16[256,1536]{1,0:T(8,128)(2,1)S(1)}, u32[]{:S(2)}) copy-start(bf16[256,1536]{1,0:T(8,128)(2,1)S(1)} %reshape.109) | copy-start | bytes 2359300
  76.6 34.8 %copy-start.5 = (f32[256,384]{1,0:T(8,128)}, f32[256,384]{1,0:T(8,128)S(1)}, u32[]{:S(2)}) copy-start(f32[256,384]{1,0:T(8,128)S(1)} %fusion.6) | copy-start | bytes 1179652
  78.7 32.7 %copy-start.7 = (f32[256,384]{1,0:T(8,128)}, f32[256,384]{1,0:T(8,128)S(1)}, u32[]{:S(2)}) copy-start(f32[256,384]{1,0:T(8,128)S(1)} %fusion.9) | copy-start | bytes 1179652
  120.5 75.3 %reduce-scatter.12.cloned.1.call-start = ((), (), s32[]{:S(2)}) async-start(), calls=%async_computation.12 | async-start | bytes 1474560
  129.5 16.1 %copy-start.4 = (bf16[256,1536]{1,0:T(8,128)(2,1)S(1)}, bf16[256,1536]{1,0:T(8,128)(2,1)}, u32[]{:S(2)}) copy-start(bf16[256,1536]{1,0:T(8,128)(2,1)} %copy-done.3) | copy-start | bytes 2359300
  129.5 16.1 %copy-start.6 = (f32[256,384]{1,0:T(8,128)S(1)}, f32[256,384]{1,0:T(8,128)}, u32[]{:S(2)}) copy-start(f32[256,384]{1,0:T(8,128)} %copy-done.5) | copy-start | bytes 1179652
  130.4 26.7 %all-to-all-start.3 = ((bf16[128,1,2]{2,1,0:T(2,128)(2,1)}), bf16[128,1,2]{2,1,0:T(2,128)(2,1)S(1)}, u32[]{:S(2)}, u32[]{:S(2)}) async-start(bf16[128,1,2]{2,1,0:T(2,128)(2,1)} %convert_element_type.114), calls=%async_computation.3 | async-start | bytes 131072 | tf_op jit(solution)/shard_map/all_to_all | solution.py:77
  145.6 69.3 %reduce-scatter.8.cloned.1.call-start = ((), (), s32[]{:S(2)}) async-start(), calls=%async_computation.10 | async-start | bytes 1474560 | tf_op jit(solution)/shard_map/reduce_scatter | solution.py:97
  148.4 1.3 copy-start.2
  149.7 1.3 copy-start.1
  157.1 34.6 %all-to-all-start.2 = ((bf16[128,2,1536]{2,1,0:T(2,128)(2,1)}), bf16[128,2,1536]{2,1,0:T(2,128)(2,1)S(1)}, u32[]{:S(2)}, u32[]{:S(2)}) async-start(bf16[128,2,1536]{2,1,0:T(2,128)(2,1)} %reshape.110), calls=%async_computation.2 | async-start | bytes 1572864 | tf_op jit(solution)/shard_map/all_to_all | solution.py:70
Sparse Core Ops, SparseCore 0:
  10.1 34.2 all-gather.7
  46.5 30.3 all-gather.5
  79.0 30.3 all-gather.3
  120.6 29.8 reduce-scatter.9
  153.2 29.1 reduce-scatter.11
  185.7 29.1 reduce-scatter.7
where the time goes:
time: 223 us; the launch traced here: 222 us
  waiting for transfers between devices  110 us (49%)
  starting transfers between devices  49.1 us (22%)
  local copies, waits for them, and re-layouts  33.3 us (15%)
  between operations  14.4 us (6%)
  matrix products  12.9 us (6%)
  other arithmetic  2.39 us (1%)
    all_gather x1, waiting for transfers between devices, shards(): lax.all_gather(w_down, 'dp', axis=1, tiled=True)  30.6 us
    all_to_all x1, waiting for transfers between devices, shards(): lax.all_to_all(send_rows, 'expert', split_axis=0, concat_axis=0, tiled=True)  24 us
    unnamed x27, local copies, waits for them, and re-layouts  23.2 us
    all_to_all x1, waiting for transfers between devices, shards(): lax.all_to_all(row_grad.reshape(experts_here, capacity, width), 'expert',...  22.8 us
    all_to_all x1, starting transfers between devices, shards(): lax.all_to_all(send_prob.astype(jnp.bfloat16), 'expert', split_axis=0, co...  18.4 us
    reduce_scatter x1, waiting for transfers between devices, shards(): lax.psum_scatter(part_down[None].astype(jnp.bfloat16), 'dp', scatter_dime...  17.1 us
    all_to_all x1, starting transfers between devices, shards(): lax.all_to_all(row_prob.reshape(experts_here, capacity).astype(jnp.bfloat...  15.2 us
    all_to_all x1, starting transfers between devices, shards(): lax.all_to_all(row_grad.reshape(experts_here, capacity, width), 'expert',...  9.44 us
  transfers between devices with their start and end apart: 10, of which 7 were waited for; matrix products, arithmetic and copies ran while one was open for 16% of the time, Pallas kernels for 0%

commit v1 on v0

v1 whole, which is shorter than its diff:
```python
import jax
import jax.numpy as jnp
from jax import lax
from jax.experimental import pallas as pl
from jax.experimental.pallas import tpu as pltpu
from jax.sharding import PartitionSpec as P

TOP = 8
EXTRA = 128
BF = jnp.bfloat16
F32 = jnp.float32
PRE_COST = 10000 << 20
PARTS_COST = 10 << 20
ADD_COST = 4000 << 20
VMEM_LIMIT = 14 * 1024 * 1024


def dot(a, b):
    return jnp.dot(a, b, preferred_element_type=F32)


def dot_nt(a, b):
    return lax.dot_general(a, b, (((1,), (1,)), ((), ())), preferred_element_type=F32)


def dot_tn(a, b):
    return lax.dot_general(a, b, (((0,), (0,)), ((), ())), preferred_element_type=F32)


def call(body, outs, args, scratch=(), cost=(0, 0)):
    vmem = pl.BlockSpec(memory_space=pltpu.VMEM)
    return pl.pallas_call(
        body,
        out_shape=[jax.ShapeDtypeStruct(s, d) for s, d in outs],
        in_specs=[vmem] * len(args),
        out_specs=[vmem] * len(outs),
        scratch_shapes=list(scratch),
        compiler_params=pltpu.CompilerParams(vmem_limit_bytes=VMEM_LIMIT),
        cost_estimate=pl.CostEstimate(flops=cost[0], bytes_accessed=cost[1], transcendentals=0),
    )(*args)


def places(routes_t, slots, capacity):
    top, toks = routes_t.shape
    row = lax.broadcasted_iota(jnp.int32, (slots, toks), 0)
    expert = row // capacity
    hits = [routes_t[k : k + 1, :] == expert for k in range(top)]
    named = sum(h.astype(F32) for h in hits)
    before = (
        lax.broadcasted_iota(jnp.int32, (toks, toks), 0)
        < lax.broadcasted_iota(jnp.int32, (toks, toks), 1)
    ).astype(BF)
    rank = dot(named.astype(BF), before)
    mine = (named > 0.5) & (rank == (row - expert * capacity).astype(F32))
    return mine, hits


def build_kernel(routes_ref, probs_ref, grad_ref, out_ref):
    experts, capacity, width = out_ref.shape
    slots = experts * capacity
    mine, hits = places(routes_ref[...], slots, capacity)
    probs = probs_ref[...]
    weight = jnp.zeros(mine.shape, F32)
    for k, hit in enumerate(hits):
        weight = weight + jnp.where(hit, probs[k : k + 1, :], 0.0)
    weight = jnp.where(mine, weight, 0.0)
    high = weight.astype(BF)
    low = (weight - high.astype(F32)).astype(BF)
    grad = grad_ref[...]
    rows = (dot(high, grad) + dot(low, grad)).astype(BF)
    out_ref[...] = rows.reshape(experts, capacity, width)


def combine_kernel(routes_ref, probs_ref, back_ref, token_ref, prob_ref):
    experts, capacity, wide = back_ref.shape
    slots, width = experts * capacity, token_ref.shape[1]
    back = back_ref[...].reshape(slots, wide)
    mine, hits = places(routes_ref[...], slots, capacity)
    token_ref[...] = dot_tn(mine.astype(BF), back[:, :width]).astype(BF)
    value = jnp.sum(back[:, width:].astype(F32), axis=1, keepdims=True)
    probs = probs_ref[...]
    for k, hit in enumerate(hits):
        got = jnp.sum(jnp.where(hit & mine, value, 0.0), axis=0, keepdims=True)
        prob_ref[k : k + 1, :] = got / probs[k : k + 1, :]


def pack_kernel(a_ref, b_ref, c_ref, out_ref):
    n = a_ref.shape[0]
    out_ref[0:n, :] = a_ref[...]
    out_ref[n : 2 * n, :] = b_ref[...]
    out_ref[2 * n :, :] = c_ref[...]


def pieces(which, own_ref, right_ref, left_ref, first_ref, second_ref):
    n = own_ref.shape[0] // 3
    lo, hi, half = which * n, (which + 1) * n, first_ref.shape[0]
    if hi <= half:
        far = first_ref[lo:hi, :]
    elif lo >= half:
        far = second_ref[lo - half : hi - half, :]
    else:
        far = jnp.concatenate([first_ref[lo:half, :], second_ref[0 : hi - half, :]], axis=0)
    return ((0, own_ref[lo:hi, :]), (3, right_ref[lo:hi, :]), (1, left_ref[lo:hi, :]), (2, far))


def columns(offset, n):
    source = lax.rem(lax.axis_index("dp") + offset, 4)
    return pl.ds(pl.multiple_of(source * n, 128), n)


def contract(rows_ref, parts):
    total = None
    for offset, block in parts:
        term = dot(rows_ref[:, columns(offset, block.shape[0])], block)
        total = term if total is None else total + term
    return total


def pre_kernel(x_ref, own_ref, right_ref, left_ref, first_ref, second_ref, gate_ref, up_ref):
    weights = (own_ref, right_ref, left_ref, first_ref, second_ref)
    gate_ref[...] = contract(x_ref, pieces(0, *weights))
    up_ref[...] = contract(x_ref, pieces(1, *weights))


def middle_kernel(
    x_ref, rows_ref, gate_ref, up_ref, own_ref, right_ref, left_ref, first_ref, second_ref,
    row_ref, g_ref, dgate_ref, dup_ref, hidden_ref, far_a_ref, far_b_ref, row_scratch,
):
    weights = (own_ref, right_ref, left_ref, first_ref, second_ref)
    n = own_ref.shape[0] // 3
    width = x_ref.shape[1]
    half = far_a_ref.shape[0]
    g_ref[...] = rows_ref[...].reshape(g_ref.shape)
    dh = contract(g_ref, pieces(2, *weights))
    gate, up = gate_ref[...], up_ref[...]
    sig = jax.nn.sigmoid(gate)
    act = gate * sig
    hidden = act * up
    row_prob = jnp.sum(hidden * dh, axis=1, keepdims=True)
    d_up = (dh * act).astype(BF)
    d_gate = (dh * up * sig * (1.0 + gate * (1.0 - sig))).astype(BF)
    hidden = hidden.astype(BF)
    dgate_ref[...] = d_gate
    dup_ref[...] = d_up
    hidden_ref[...] = hidden
    far = columns(2, n)
    far_a_ref[0:n, :] = dot_tn(x_ref[:, far], d_gate).astype(BF)
    part_up = dot_tn(x_ref[:, far], d_up).astype(BF)
    far_a_ref[n:half, :] = part_up[0 : half - n, :]
    far_b_ref[0 : 2 * n - half, :] = part_up[half - n :, :]
    far_b_ref[2 * n - half :, :] = dot_tn(g_ref[:, far], hidden).astype(BF)
    for (offset, g_block), (_, u_block) in zip(pieces(0, *weights), pieces(1, *weights)):
        row_scratch[:, columns(offset, n)] = (dot_nt(d_gate, g_block) + dot_nt(d_up, u_block)).astype(BF)
    lane = lax.broadcasted_iota(jnp.int32, (x_ref.shape[0], EXTRA), 1)
    high = row_prob.astype(BF).astype(F32)
    row_scratch[:, width:] = jnp.where(
        lane == 0, high, jnp.where(lane == 1, row_prob - high, 0.0)
    ).astype(BF)
    row_ref[...] = row_scratch[...].reshape(row_ref.shape)


def parts_kernel(x_ref, g_ref, dgate_ref, dup_ref, hidden_ref, own_ref, right_ref, left_ref):
    n = x_ref.shape[1] // 4
    for offset, out in ((1, right_ref), (3, left_ref), (0, own_ref)):
        cols = columns(offset, n)
        out[0:n, :] = dot_tn(x_ref[:, cols], dgate_ref[...]).astype(BF)
        out[n : 2 * n, :] = dot_tn(x_ref[:, cols], dup_ref[...]).astype(BF)
        out[2 * n :, :] = dot_tn(g_ref[:, cols], hidden_ref[...]).astype(BF)


def add_kernel(right_ref, left_ref, from_left_ref, from_right_ref, to_right_ref, to_left_ref):
    half = from_left_ref.shape[0]
    to_right_ref[0:half, :] = (
        right_ref[0:half, :].astype(F32) + from_left_ref[...].astype(F32)
    ).astype(BF)
    to_right_ref[half:, :] = right_ref[half:, :]
    to_left_ref[0:half, :] = left_ref[0:half, :]
    to_left_ref[half:, :] = (
        left_ref[half:, :].astype(F32) + from_right_ref[...].astype(F32)
    ).astype(BF)


def sum_kernel(own_ref, a_ref, b_ref, gate_ref, up_ref, down_ref):
    n = gate_ref.shape[0]
    for i, out in enumerate((gate_ref, up_ref, down_ref)):
        at = slice(i * n, (i + 1) * n)
        out[...] = (
            own_ref[at, :].astype(F32) + a_ref[at, :].astype(F32) + b_ref[at, :].astype(F32)
        ).astype(BF)


def shift(value, by):
    return lax.ppermute(value, "dp", [(i, (i + by) % 4) for i in range(4)])


def shards(out_grad, routes, gate_probs, saved_inputs, w_gate, w_up, w_down):
    toks, width = out_grad.shape
    experts = lax.axis_size("expert")
    slots = saved_inputs.shape[2]
    capacity = slots // experts
    n, f = w_gate.shape[1], w_gate.shape[2]
    half = 3 * n // 2
    x = saved_inputs[0, 0]
    routes_t, probs_t = routes.T, gate_probs.T

    (own,) = call(pack_kernel, [((3 * n, f), BF)], (w_gate[0], w_up[0], w_down[0]), cost=(0, 12 * n * f))
    right = shift(own, 1)
    left = shift(own, -1)
    (send,) = call(
        build_kernel,
        [((experts, capacity, width), BF)],
        (routes_t, probs_t, out_grad),
        cost=(0, 2 * slots * width),
    )
    rows = lax.all_to_all(send, "expert", split_axis=0, concat_axis=0, tiled=True)
    first = shift(right[:half], 1)
    second = shift(left[half:], -1)
    weights = (own, right, left, first, second)
    pre_gate, pre_up = call(
        pre_kernel, [((slots, f), F32)] * 2, (x, *weights), cost=(PRE_COST, 0)
    )
    row_grad, g, d_gate, d_up, hidden, far_a, far_b = call(
        middle_kernel,
        [((experts, capacity, width + EXTRA), BF), ((slots, width), BF)]
        + [((slots, f), BF)] * 3
        + [((half, f), BF)] * 2,
        (x, rows, pre_gate, pre_up, *weights),
        scratch=[pltpu.VMEM((slots, width + EXTRA), BF)],
        cost=(8 * slots * width * f, 8 << 20),
    )
    from_left = shift(far_a, 1)
    from_right = shift(far_b, -1)
    back = lax.all_to_all(row_grad, "expert", split_axis=0, concat_axis=0, tiled=True)
    mine, to_right, to_left = call(
        parts_kernel,
        [((3 * n, f), BF)] * 3,
        (x, g, d_gate, d_up, hidden),
        cost=(PARTS_COST, 0),
    )
    to_right, to_left = call(
        add_kernel, [((3 * n, f), BF)] * 2, (to_right, to_left, from_left, from_right), cost=(ADD_COST, 0)
    )
    a = shift(to_right, 1)
    b = shift(to_left, -1)
    grads = call(sum_kernel, [((n, f), BF)] * 3, (mine, a, b), cost=(ADD_COST, 0))
    token_grad, prob_t = call(
        combine_kernel,
        [((toks, width), BF), (probs_t.shape, F32)],
        (routes_t, probs_t, back),
        cost=(0, 1 << 20),
    )
    return (token_grad, prob_t.T, grads[0][None], grads[1][None], grads[2][None])


def solution(mesh):
    return jax.shard_map(
        shards,
        mesh=mesh,
        in_specs=(
            P(("dp", "expert"), None),
            P(("dp", "expert"), None),
            P(("dp", "expert"), None),
            P("dp", "expert", None, None),
            P("expert", "dp", None),
            P("expert", "dp", None),
            P("expert", "dp", None),
        ),
        out_specs=(
            P(("dp", "expert"), None),
            P(("dp", "expert"), None),
            P("expert", "dp", None),
            P("expert", "dp", None),
            P("expert", "dp", None),
        ),
        check_vma=False,
    )
```

time: 223 us -> 121 us (0.54)
  the two profiles are of different devices: /device:TPU:1 before, /device:TPU:14 now
where the time goes in v1:
time: 121 us; the launch traced here: 120 us
  starting transfers between devices  58 us (48%)
  waiting for transfers between devices  34.8 us (29%)
  local copies, waits for them, and re-layouts  14.2 us (12%)
  Pallas kernels  12.5 us (10%)
    ppermute x8, waiting for transfers between devices, shift(): return lax.ppermute(value, 'dp', [(i, (i + by) % 4) for i in range(4)])  32 us
    ppermute x8, starting transfers between devices, shift(): return lax.ppermute(value, 'dp', [(i, (i + by) % 4) for i in range(4)])  27.1 us
    all_to_all x1, starting transfers between devices, shards(): lax.all_to_all(send, 'expert', split_axis=0, concat_axis=0, tiled=True)  17.4 us
    all_to_all x1, starting transfers between devices, shards(): lax.all_to_all(row_grad, 'expert', split_axis=0, concat_axis=0, tiled=True)  13.5 us
    unnamed x44, local copies, waits for them, and re-layouts  13.1 us
    pallas_call x8, Pallas kernels, call(): pl.pallas_call(body, out_shape=[jax.ShapeDtypeStruct(s, d) for s, d in ou...  12.5 us
    all_to_all x1, waiting for transfers between devices, shards(): lax.all_to_all(send, 'expert', split_axis=0, concat_axis=0, tiled=True)  2.74 us
  transfers between devices with their start and end apart: 10, of which 5 were waited for; matrix products, arithmetic and copies ran while one was open for 1% of the time, Pallas kernels for 6%

profile of v1, /device:TPU:14, one launch (start us, length us, event | category | flops | bytes accessed | tf_op | source)
XLA Modules:
  0.0 120.4 jit_solution(16065967592484749968)
XLA Ops:
  3.6 2.7 %collective-permute-start.1 = (bf16[1152,384]{1,0:T(8,128)(2,1)S(1)}, bf16[1152,384]{1,0:T(8,128)(2,1)S(1)}, u32[]{:S(2)}, u32[]{:S(2)}) collective-permute-start(bf16[1152,384]{1,0:T(8,128)(2,1)S(1)} %shard_map.111.own_ref), channel_id=1, source_target_pairs={{0,384},{128,0},{256,128},{384,256},{1,385},{129,1},{257,129},{385... | collective-permute-start | bytes 2654216 | tf_op jit(solution)/shard_map/ppermute | solution.py:193
  6.4 4.3 %collective-permute-start = (bf16[1152,384]{1,0:T(8,128)(2,1)S(1)}, bf16[1152,384]{1,0:T(8,128)(2,1)}, u32[]{:S(2)}, u32[]{:S(2)}) collective-permute-start(bf16[1152,384]{1,0:T(8,128)(2,1)S(1)} %shard_map.111.own_ref), channel_id=1, source_target_pairs={{0,128},{128,256},{256,384},{384,0},{1,129},{129,257},{257,385},{3... | collective-permute-start | bytes 2654216 | tf_op jit(solution)/shard_map/ppermute | solution.py:193
  10.7 1.6 %shard_map.110 = bf16[128,2,1536]{2,1,0:T(2,128)(2,1)} custom-call(s32[8,16]{1,0:T(8,128)S(1)} %bitcast.16, f32[8,16]{1,0:T(8,128)S(1)} %bitcast.18, bf16[16,1536]{1,0:T(8,128)(2,1)S(1)} %copy-done.19), custom_call_target="tpu_custom_call" | custom-call | bytes 786432 | tf_op jit(solution)/shard_map/pallas_call | solution.py:32
  12.3 17.4 %all-to-all-start = ((bf16[128,2,1536]{2,1,0:T(2,128)(2,1)}), bf16[128,2,1536]{2,1,0:T(2,128)(2,1)S(1)}, u32[]{:S(2)}, u32[]{:S(2)}) async-start(bf16[128,2,1536]{2,1,0:T(2,128)(2,1)} %shard_map.110), calls=%async_computation | async-start | bytes 1572864 | tf_op jit(solution)/shard_map/all_to_all | solution.py:215
  29.8 2.1 %collective-permute-start.3 = (bf16[576,384]{1,0:T(8,128)(2,1)S(1)}, bf16[576,384]{1,0:T(8,128)(2,1)S(1)}, u32[]{:S(2)}, u32[]{:S(2)}) collective-permute-start(bf16[576,384]{1,0:T(8,128)(2,1)S(1)} %slice.9), channel_id=1, source_target_pairs={{0,384},{128,0},{256,128},{384,256},{1,385},{129,1},{257,129},{385... | collective-permute-start | bytes 1327112 | tf_op jit(solution)/shard_map/ppermute | solution.py:193
  31.9 1.1 slice.8
  32.9 5.1 %collective-permute-start.2 = (bf16[576,384]{1,0:T(8,128)(2,1)S(1)}, bf16[576,384]{1,0:T(8,128)(2,1)S(1)}, u32[]{:S(2)}, u32[]{:S(2)}) collective-permute-start(bf16[576,384]{1,0:T(8,128)(2,1)S(1)} %slice.8), channel_id=1, source_target_pairs={{0,128},{128,256},{256,384},{384,0},{1,129},{129,257},{257,385},{3... | collective-permute-start | bytes 1327112 | tf_op jit(solution)/shard_map/ppermute | solution.py:193
  38.1 7.2 %collective-permute-done.3.second_ref = bf16[576,384]{1,0:T(8,128)(2,1)S(1)} collective-permute-done((bf16[576,384]{1,0:T(8,128)(2,1)S(1)}, bf16[576,384]{1,0:T(8,128)(2,1)S(1)}, u32[]{:S(2)}, u32[]{:S(2)}) %collective-permute-start.3) | collective-permute-done | bytes 442400 | tf_op jit(solution)/shard_map/ppermute | solution.py:193
  45.3 2.3 %collective-permute-done.2.first_ref = bf16[576,384]{1,0:T(8,128)(2,1)S(1)} collective-permute-done((bf16[576,384]{1,0:T(8,128)(2,1)S(1)}, bf16[576,384]{1,0:T(8,128)(2,1)S(1)}, u32[]{:S(2)}, u32[]{:S(2)}) %collective-permute-start.2) | collective-permute-done | bytes 442400 | tf_op jit(solution)/shard_map/ppermute | solution.py:193
  47.5 2.3 %shard_map.112 = (f32[256,384]{1,0:T(8,128)S(1)}, f32[256,384]{1,0:T(8,128)S(1)}) custom-call(bf16[256,1536]{1,0:T(8,128)(2,1)S(1)} %bitcast.10, bf16[1152,384]{1,0:T(8,128)(2,1)S(1)} %shard_map.111.own_ref, bf16[1152,384]{1,0:T(8,128)(2,1)} %collective-permute-done.right_ref, bf16[1152,384]{1,0:T(8,128)(2,1)S(1)} %collective-permute-done.1.left_ref, ...), custom_call_target="tpu_custom_call" | custom-call | flops 10485760000 | tf_op jit(solution)/shard_map/pallas_call | solution.py:32
  52.8 2.7 %all-to-all-done.rows_ref = bf16[128,2,1536]{2,1,0:T(2,128)(2,1)S(1)} async-done(((bf16[128,2,1536]{2,1,0:T(2,128)(2,1)}), bf16[128,2,1536]{2,1,0:T(2,128)(2,1)S(1)}, u32[]{:S(2)}, u32[]{:S(2)}) %all-to-all-start) | async-done | bytes 786464 | tf_op jit(solution)/shard_map/all_to_all | solution.py:215
  55.6 1.0 copy-done.5
  59.6 3.9 %shard_map.113 = (bf16[128,2,1664]{2,1,0:T(2,128)(2,1)S(1)}, bf16[256,1536]{1,0:T(8,128)(2,1)S(1)}, bf16[256,384]{1,0:T(8,128)(2,1)S(1)}, bf16[256,384]{1,0:T(8,...) custom-call(bf16[256,1536]{1,0:T(8,128)(2,1)S(1)} %bitcast.11, ...), custom_call_target="tpu_custom_call" | custom-call | flops 1207959552 | bytes 8388608 | tf_op jit(solution)/shard_map/pallas_call | solution.py:32
  66.7 2.9 %collective-permute-start.4 = (bf16[576,384]{1,0:T(8,128)(2,1)}, bf16[576,384]{1,0:T(8,128)(2,1)S(1)}, u32[]{:S(2)}, u32[]{:S(2)}) collective-permute-start(bf16[576,384]{1,0:T(8,128)(2,1)} %get-tuple-element.36), channel_id=1, source_target_pairs={{0,128},{128,256},{256,384},{384,0},{1,129},{129,257},{257,385},{3... | collective-permute-start | bytes 1327112 | tf_op jit(solution)/shard_map/ppermute | solution.py:193
  69.5 3.0 %collective-permute-start.5 = (bf16[576,384]{1,0:T(8,128)(2,1)}, bf16[576,384]{1,0:T(8,128)(2,1)}, u32[]{:S(2)}, u32[]{:S(2)}) collective-permute-start(bf16[576,384]{1,0:T(8,128)(2,1)} %get-tuple-element.37), channel_id=1, source_target_pairs={{0,384},{128,0},{256,128},{384,256},{1,385},{129,1},{257,129},{385... | collective-permute-start | bytes 1327112 | tf_op jit(solution)/shard_map/ppermute | solution.py:193
  72.5 13.5 %all-to-all-start.1 = ((bf16[128,2,1664]{2,1,0:T(2,128)(2,1)}), bf16[128,2,1664]{2,1,0:T(2,128)(2,1)S(1)}, u32[]{:S(2)}, u32[]{:S(2)}) async-start(bf16[128,2,1664]{2,1,0:T(2,128)(2,1)} %copy-done.1), calls=%async_computation.1 | async-start | bytes 1703936 | tf_op jit(solution)/shard_map/all_to_all | solution.py:233
  86.1 1.1 shard_map.115
  87.3 1.3 %shard_map.116 = (bf16[1152,384]{1,0:T(8,128)(2,1)S(1)}, bf16[1152,384]{1,0:T(8,128)(2,1)S(1)}) custom-call(bf16[1152,384]{1,0:T(8,128)(2,1)S(1)} %get-tuple-element.34.right_ref, bf16[1152,384]{1,0:T(8,128)(2,1)S(1)} %get-tuple-element.35.left_ref, bf16[576,384]{1,0:T(8,128)(2,1)S(1)} %collective-permute-done.4.from_left_ref, ...), custom_call_target="tpu_custom_call" | custom-call | flops 4194304000 | tf_op jit(solution)/shard_map/pallas_call | solution.py:32
  88.5 5.1 %collective-permute-start.6 = (bf16[1152,384]{1,0:T(8,128)(2,1)S(1)}, bf16[1152,384]{1,0:T(8,128)(2,1)S(1)}, u32[]{:S(2)}, u32[]{:S(2)}) collective-permute-start(bf16[1152,384]{1,0:T(8,128)(2,1)S(1)} %get-tuple-element.38), channel_id=1, source_target_pairs={{0,128},{128,256},{256,384},{384,0},{1,129},{129,257},{257,385},{3... | collective-permute-start | bytes 2654216 | tf_op jit(solution)/shard_map/ppermute | solution.py:193
  93.7 1.9 %collective-permute-start.7 = (bf16[1152,384]{1,0:T(8,128)(2,1)S(1)}, bf16[1152,384]{1,0:T(8,128)(2,1)S(1)}, u32[]{:S(2)}, u32[]{:S(2)}) collective-permute-start(bf16[1152,384]{1,0:T(8,128)(2,1)S(1)} %get-tuple-element.39), channel_id=1, source_target_pairs={{0,384},{128,0},{256,128},{384,256},{1,385},{129,1},{257,129},{385... | collective-permute-start | bytes 2654216 | tf_op jit(solution)/shard_map/ppermute | solution.py:193
  95.6 17.3 %collective-permute-done.6.a_ref = bf16[1152,384]{1,0:T(8,128)(2,1)S(1)} collective-permute-done((bf16[1152,384]{1,0:T(8,128)(2,1)S(1)}, bf16[1152,384]{1,0:T(8,128)(2,1)S(1)}, u32[]{:S(2)}, u32[]{:S(2)}) %collective-permute-start.6) | collective-permute-done | bytes 884768 | tf_op jit(solution)/shard_map/ppermute | solution.py:193
  112.9 5.3 %collective-permute-done.7.b_ref = bf16[1152,384]{1,0:T(8,128)(2,1)S(1)} collective-permute-done((bf16[1152,384]{1,0:T(8,128)(2,1)S(1)}, bf16[1152,384]{1,0:T(8,128)(2,1)S(1)}, u32[]{:S(2)}, u32[]{:S(2)}) %collective-permute-start.7) | collective-permute-done | bytes 884768 | tf_op jit(solution)/shard_map/ppermute | solution.py:193
  118.2 1.0 shard_map.117
  119.2 1.2 shard_map.114
  (50 shorter events, 12.2 us)
Async XLA Ops:
  0.6 1.0 copy-start.12
  1.6 1.0 copy-start.13
  2.6 1.0 copy-start.14
  3.5 7.2 %copy-start.19 = (bf16[16,1536]{1,0:T(8,128)(2,1)S(1)}, bf16[16,1536]{1,0:T(8,128)(2,1)}, u32[]{:S(2)}) copy-start(bf16[16,1536]{1,0:T(8,128)(2,1)} %grad_ref.1) | copy-start | bytes 147460
  3.5 7.2 %copy-start.20 = (s32[16,8]{0,1:T(8,128)S(1)}, s32[16,8]{0,1:T(8,128)}, u32[]{:S(2)}) copy-start(s32[16,8]{0,1:T(8,128)} %param.8) | copy-start | bytes 1540
  3.5 7.2 %copy-start.21 = (f32[16,8]{0,1:T(8,128)S(1)}, f32[16,8]{0,1:T(8,128)}, u32[]{:S(2)}) copy-start(f32[16,8]{0,1:T(8,128)} %param.9) | copy-start | bytes 1540
  3.6 26.1 %collective-permute-start.1 = (bf16[1152,384]{1,0:T(8,128)(2,1)S(1)}, bf16[1152,384]{1,0:T(8,128)(2,1)S(1)}, u32[]{:S(2)}, u32[]{:S(2)}) collective-permute-start(bf16[1152,384]{1,0:T(8,128)(2,1)S(1)} %shard_map.111.own_ref), channel_id=1, source_target_pairs={{0,384},{128,0},{256,128},{384,256},{1,385},{129,1},{257,129},{385... | collective-permute-start | bytes 2654216 | tf_op jit(solution)/shard_map/ppermute | solution.py:193
  6.4 25.5 %collective-permute-start = (bf16[1152,384]{1,0:T(8,128)(2,1)S(1)}, bf16[1152,384]{1,0:T(8,128)(2,1)}, u32[]{:S(2)}, u32[]{:S(2)}) collective-permute-start(bf16[1152,384]{1,0:T(8,128)(2,1)S(1)} %shard_map.111.own_ref), channel_id=1, source_target_pairs={{0,128},{128,256},{256,384},{384,0},{1,129},{129,257},{257,385},{3... | collective-permute-start | bytes 2654216 | tf_op jit(solution)/shard_map/ppermute | solution.py:193
  12.3 43.2 %all-to-all-start = ((bf16[128,2,1536]{2,1,0:T(2,128)(2,1)}), bf16[128,2,1536]{2,1,0:T(2,128)(2,1)S(1)}, u32[]{:S(2)}, u32[]{:S(2)}) async-start(bf16[128,2,1536]{2,1,0:T(2,128)(2,1)} %shard_map.110), calls=%async_computation | async-start | bytes 1572864 | tf_op jit(solution)/shard_map/all_to_all | solution.py:215
  29.7 17.8 %copy-start = (bf16[1,1,256,1536]{3,2,1,0:T(8,128)(2,1)S(1)}, bf16[1,1,256,1536]{3,2,1,0:T(8,128)(2,1)}, u32[]{:S(2)}) copy-start(bf16[1,1,256,1536]{3,2,1,0:T(8,128)(2,1)} %param.10) | copy-start | bytes 2359300
  29.8 15.5 %collective-permute-start.3 = (bf16[576,384]{1,0:T(8,128)(2,1)S(1)}, bf16[576,384]{1,0:T(8,128)(2,1)S(1)}, u32[]{:S(2)}, u32[]{:S(2)}) collective-permute-start(bf16[576,384]{1,0:T(8,128)(2,1)S(1)} %slice.9), channel_id=1, source_target_pairs={{0,384},{128,0},{256,128},{384,256},{1,385},{129,1},{257,129},{385... | collective-permute-start | bytes 1327112 | tf_op jit(solution)/shard_map/ppermute | solution.py:193
  32.9 14.6 %collective-permute-start.2 = (bf16[576,384]{1,0:T(8,128)(2,1)S(1)}, bf16[576,384]{1,0:T(8,128)(2,1)S(1)}, u32[]{:S(2)}, u32[]{:S(2)}) collective-permute-start(bf16[576,384]{1,0:T(8,128)(2,1)S(1)} %slice.8), channel_id=1, source_target_pairs={{0,128},{128,256},{256,384},{384,0},{1,129},{129,257},{257,385},{3... | collective-permute-start | bytes 1327112 | tf_op jit(solution)/shard_map/ppermute | solution.py:193
  55.6 1.0 copy-start.5
  56.6 1.0 copy-start.7
  57.6 1.0 copy-start.9
  58.6 1.0 copy-start.11
  66.7 20.6 %collective-permute-start.4 = (bf16[576,384]{1,0:T(8,128)(2,1)}, bf16[576,384]{1,0:T(8,128)(2,1)S(1)}, u32[]{:S(2)}, u32[]{:S(2)}) collective-permute-start(bf16[576,384]{1,0:T(8,128)(2,1)} %get-tuple-element.36), channel_id=1, source_target_pairs={{0,128},{128,256},{256,384},{384,0},{1,129},{129,257},{257,385},{3... | collective-permute-start | bytes 1327112 | tf_op jit(solution)/shard_map/ppermute | solution.py:193
  69.5 17.7 %collective-permute-start.5 = (bf16[576,384]{1,0:T(8,128)(2,1)}, bf16[576,384]{1,0:T(8,128)(2,1)}, u32[]{:S(2)}, u32[]{:S(2)}) collective-permute-start(bf16[576,384]{1,0:T(8,128)(2,1)} %get-tuple-element.37), channel_id=1, source_target_pairs={{0,384},{128,0},{256,128},{384,256},{1,385},{129,1},{257,129},{385... | collective-permute-start | bytes 1327112 | tf_op jit(solution)/shard_map/ppermute | solution.py:193
  72.5 13.6 %copy-start.3 = (bf16[256,1536]{1,0:T(8,128)(2,1)S(1)}, bf16[256,1536]{1,0:T(8,128)(2,1)}, u32[]{:S(2)}) copy-start(bf16[256,1536]{1,0:T(8,128)(2,1)} %copy-done.2) | copy-start | bytes 2359300
  72.5 13.6 %copy-start.16 = (bf16[256,384]{1,0:T(8,128)(2,1)S(1)}, bf16[256,384]{1,0:T(8,128)(2,1)}, u32[]{:S(2)}) copy-start(bf16[256,384]{1,0:T(8,128)(2,1)} %copy-done.15) | copy-start | bytes 589828
  72.5 13.6 %copy-start.18 = (bf16[256,384]{1,0:T(8,128)(2,1)S(1)}, bf16[256,384]{1,0:T(8,128)(2,1)}, u32[]{:S(2)}) copy-start(bf16[256,384]{1,0:T(8,128)(2,1)} %copy-done.17) | copy-start | bytes 589828
  72.5 46.7 %all-to-all-start.1 = ((bf16[128,2,1664]{2,1,0:T(2,128)(2,1)}), bf16[128,2,1664]{2,1,0:T(2,128)(2,1)S(1)}, u32[]{:S(2)}, u32[]{:S(2)}) async-start(bf16[128,2,1664]{2,1,0:T(2,128)(2,1)} %copy-done.1), calls=%async_computation.1 | async-start | bytes 1703936 | tf_op jit(solution)/shard_map/all_to_all | solution.py:233
  88.5 24.3 %collective-permute-start.6 = (bf16[1152,384]{1,0:T(8,128)(2,1)S(1)}, bf16[1152,384]{1,0:T(8,128)(2,1)S(1)}, u32[]{:S(2)}, u32[]{:S(2)}) collective-permute-start(bf16[1152,384]{1,0:T(8,128)(2,1)S(1)} %get-tuple-element.38), channel_id=1, source_target_pairs={{0,128},{128,256},{256,384},{384,0},{1,129},{129,257},{257,385},{3... | collective-permute-start | bytes 2654216 | tf_op jit(solution)/shard_map/ppermute | solution.py:193
  93.7 24.5 %collective-permute-start.7 = (bf16[1152,384]{1,0:T(8,128)(2,1)S(1)}, bf16[1152,384]{1,0:T(8,128)(2,1)S(1)}, u32[]{:S(2)}, u32[]{:S(2)}) collective-permute-start(bf16[1152,384]{1,0:T(8,128)(2,1)S(1)} %get-tuple-element.39), channel_id=1, source_target_pairs={{0,384},{128,0},{256,128},{384,256},{1,385},{129,1},{257,129},{385... | collective-permute-start | bytes 2654216 | tf_op jit(solution)/shard_map/ppermute | solution.py:193
  (8 other events, 6.2 us)

commit v2 on v1

v2 whole, which is shorter than its diff:
```python
import jax
import jax.numpy as jnp
from jax import lax
from jax.experimental import pallas as pl
from jax.experimental.pallas import tpu as pltpu
from jax.sharding import PartitionSpec as P

TOP = 8
EXTRA = 128
BF = jnp.bfloat16
F32 = jnp.float32
PRE_COST = 12000 << 20
SUM_COST = 12000 << 20


def dot(a, b):
    return jnp.dot(a, b, preferred_element_type=F32)


def dot_nt(a, b):
    return lax.dot_general(a, b, (((1,), (1,)), ((), ())), preferred_element_type=F32)


def dot_tn(a, b):
    return lax.dot_general(a, b, (((0,), (0,)), ((), ())), preferred_element_type=F32)


def call(body, outs, args, scratch=(), flops=0, where=pltpu.HBM, mib=61):
    spec = pl.BlockSpec(memory_space=where)
    return pl.pallas_call(
        body,
        out_shape=[jax.ShapeDtypeStruct(s, d) for s, d in outs],
        in_specs=[spec] * len(args),
        out_specs=[spec] * len(outs),
        scratch_shapes=list(scratch),
        compiler_params=pltpu.CompilerParams(vmem_limit_bytes=mib * 1024 * 1024),
        cost_estimate=pl.CostEstimate(flops=flops, bytes_accessed=0, transcendentals=0),
    )(*args)


def start(copies, sems):
    made = [pltpu.make_async_copy(a, b, sems.at[i]) for i, (a, b) in enumerate(copies)]
    for c in made:
        c.start()
    return made


def finish(copies):
    for c in copies:
        c.wait()


def places(routes_t, slots, capacity):
    top, toks = routes_t.shape
    row = lax.broadcasted_iota(jnp.int32, (slots, toks), 0)
    expert = row // capacity
    hits = [routes_t[k : k + 1, :] == expert for k in range(top)]
    named = sum(h.astype(F32) for h in hits)
    before = (
        lax.broadcasted_iota(jnp.int32, (toks, toks), 0)
        < lax.broadcasted_iota(jnp.int32, (toks, toks), 1)
    ).astype(BF)
    rank = dot(named.astype(BF), before)
    mine = (named > 0.5) & (rank == (row - expert * capacity).astype(F32))
    return mine, hits


def build_kernel(routes_ref, probs_ref, grad_ref, out_ref):
    experts, capacity, width = out_ref.shape
    slots = experts * capacity
    mine, hits = places(routes_ref[...], slots, capacity)
    probs = probs_ref[...]
    weight = jnp.zeros(mine.shape, F32)
    for k, hit in enumerate(hits):
        weight = weight + jnp.where(hit, probs[k : k + 1, :], 0.0)
    weight = jnp.where(mine, weight, 0.0)
    high = weight.astype(BF)
    low = (weight - high.astype(F32)).astype(BF)
    grad = grad_ref[...]
    rows = (dot(high, grad) + dot(low, grad)).astype(BF)
    out_ref[...] = rows.reshape(experts, capacity, width)


def combine_kernel(routes_ref, probs_ref, back_ref, token_ref, prob_ref):
    experts, capacity, wide = back_ref.shape
    slots, width = experts * capacity, token_ref.shape[1]
    back = back_ref[...].reshape(slots, wide)
    mine, hits = places(routes_ref[...], slots, capacity)
    token_ref[...] = dot_tn(mine.astype(BF), back[:, :width]).astype(BF)
    value = jnp.sum(back[:, width:].astype(F32), axis=1, keepdims=True)
    probs = probs_ref[...]
    for k, hit in enumerate(hits):
        got = jnp.sum(jnp.where(hit & mine, value, 0.0), axis=0, keepdims=True)
        prob_ref[k : k + 1, :] = got / probs[k : k + 1, :]


def pack_kernel(a_ref, b_ref, c_ref, out_hbm, out_ref, sems):
    n = a_ref.shape[0]
    blocks = [pl.ds(i * n, n) for i in range(3)]
    copies = start([(r, out_ref.at[at, :]) for r, at in zip((a_ref, b_ref, c_ref), blocks)], sems)
    out = []
    for i, at in enumerate(blocks):
        copies[i].wait()
        out += start([(out_ref.at[at, :], out_hbm.at[at, :])], sems.at[pl.ds(3 + i, 1)])
    finish(out)


def span(offset, n):
    source = lax.rem(lax.axis_index("dp") + offset, 4)
    return pl.ds(pl.multiple_of(source * n, 128), n)


def pre_kernel(x_hbm, own, far, acc_hbm, x_ref, w_ref, acc_ref, sems):
    n, f = own.shape[0] // 3, own.shape[1]
    moves = []
    for i, (offset, block) in enumerate(((0, own), (2, far))):
        at = pl.ds(i * n, n)
        moves.append((x_hbm.at[:, span(offset, n)], x_ref.at[:, at]))
        moves.append((block.at[pl.ds(0, n), :], w_ref.at[at, pl.ds(0, f)]))
        moves.append((block.at[pl.ds(n, n), :], w_ref.at[at, pl.ds(f, f)]))
    finish(start(moves, sems))
    acc_ref[...] = dot(x_ref[...], w_ref[...])
    finish(start([(acc_ref, acc_hbm)], sems))


def middle_kernel(
    x_hbm, rows_hbm, acc_hbm, own, right, left, far,
    back_hbm, to_own, to_right, to_left, to_far,
    x_ref, rows_ref, acc_ref, w_ref, wd_ref, g_ref, row_ref, back_ref, part_ref, sems,
):
    width, n, f = x_ref.shape[1], x_ref.shape[1] // 4, wd_ref.shape[1]
    moves = [(rows_hbm, rows_ref), (x_hbm, x_ref), (acc_hbm, acc_ref)]
    for offset, block in ((3, right), (1, left), (0, own), (2, far)):
        at = span(offset, n)
        moves.append((block.at[pl.ds(0, n), :], w_ref.at[at, pl.ds(0, f)]))
        moves.append((block.at[pl.ds(n, n), :], w_ref.at[at, pl.ds(f, f)]))
        moves.append((block.at[pl.ds(2 * n, n), :], wd_ref.at[at, :]))
    copies = start(moves, sems)
    finish(copies[0:1])
    g_ref[...] = rows_ref[...].reshape(g_ref.shape)
    finish(copies[1:])
    pre = acc_ref[...]
    for offset in (3, 1):
        pre = pre + dot(x_ref[:, span(offset, n)], w_ref[span(offset, n), :])
    dh = dot(g_ref[...], wd_ref[...])
    gate, up = pre[:, :f], pre[:, f:]
    sig = jax.nn.sigmoid(gate)
    act = gate * sig
    hidden = act * up
    row_prob = jnp.sum(hidden * dh, axis=1, keepdims=True)
    d_up = (dh * act).astype(BF)
    d_gate = (dh * up * sig * (1.0 + gate * (1.0 - sig))).astype(BF)
    hidden = hidden.astype(BF)
    both = jnp.concatenate([d_gate, d_up], axis=1)
    out = []
    for k, (offset, to) in enumerate(((2, to_far), (1, to_right), (3, to_left), (0, to_own))):
        cols = span(offset, n)
        part = dot_tn(x_ref[:, cols], both).astype(BF)
        part_ref[k, 0:n, :] = part[:, :f]
        part_ref[k, n : 2 * n, :] = part[:, f:]
        part_ref[k, 2 * n :, :] = dot_tn(g_ref[:, cols], hidden).astype(BF)
        out += start([(part_ref.at[k], to)], sems.at[pl.ds(15 + k, 1)])
    for i in range(4):
        at = slice(i * n, (i + 1) * n)
        row_ref[:, at] = dot_nt(both, w_ref[at, :]).astype(BF)
    lane = lax.broadcasted_iota(jnp.int32, (x_ref.shape[0], EXTRA), 1)
    high = row_prob.astype(BF).astype(F32)
    row_ref[:, width:] = jnp.where(
        lane == 0, high, jnp.where(lane == 1, row_prob - high, 0.0)
    ).astype(BF)
    back_ref[...] = row_ref[...].reshape(back_ref.shape)
    out += start([(back_ref, back_hbm)], sems.at[pl.ds(19, 1)])
    finish(out)


def first_sum_kernel(own, far, sum_hbm, in_ref, sum_ref, sems):
    finish(start([(own, in_ref.at[0]), (far, in_ref.at[1])], sems))
    sum_ref[...] = in_ref[0].astype(F32) + in_ref[1].astype(F32)
    finish(start([(sum_ref, sum_hbm)], sems))


def last_sum_kernel(sum_hbm, a, b, gate_hbm, up_hbm, down_hbm, sum_ref, in_ref, out_ref, sems):
    n = gate_hbm.shape[0]
    blocks = [pl.ds(i * n, n) for i in range(3)]
    moves = []
    for at in blocks:
        moves += [(sum_hbm.at[at, :], sum_ref.at[at, :])]
        moves += [(r.at[at, :], in_ref.at[k, at, :]) for k, r in enumerate((a, b))]
    copies = start(moves, sems)
    out = []
    for i, hbm in enumerate((gate_hbm, up_hbm, down_hbm)):
        finish(copies[3 * i : 3 * i + 3])
        at = blocks[i]
        out_ref[at, :] = (
            sum_ref[at, :] + in_ref[0, at, :].astype(F32) + in_ref[1, at, :].astype(F32)
        ).astype(BF)
        out += start([(out_ref.at[at, :], hbm)], sems.at[pl.ds(9 + i, 1)])
    finish(out)


def shift(value, by):
    return lax.ppermute(value, "dp", [(i, (i + by) % 4) for i in range(4)])


def shards(out_grad, routes, gate_probs, saved_inputs, w_gate, w_up, w_down):
    toks, width = out_grad.shape
    experts = lax.axis_size("expert")
    slots = saved_inputs.shape[2]
    capacity = slots // experts
    n, f = w_gate.shape[1], w_gate.shape[2]
    x = saved_inputs[0, 0]
    routes_t, probs_t = routes.T, gate_probs.T
    dma = pltpu.SemaphoreType.DMA
    block = ((3 * n, f), BF)
    row_block = (experts, capacity, width + EXTRA)

    (own,) = call(
        pack_kernel, [block], (w_gate[0], w_up[0], w_down[0]), [pltpu.VMEM(*block), dma((6,))]
    )
    far = shift(own, 2)
    (send,) = call(
        build_kernel,
        [((experts, capacity, width), BF)],
        (routes_t, probs_t, out_grad),
        where=pltpu.VMEM,
        mib=16,
    )
    rows = lax.all_to_all(send, "expert", split_axis=0, concat_axis=0, tiled=True)
    right = shift(own, 1)
    left = shift(own, -1)
    (acc,) = call(
        pre_kernel,
        [((slots, 2 * f), F32)],
        (x, own, far),
        [
            pltpu.VMEM((slots, 2 * n), BF),
            pltpu.VMEM((2 * n, 2 * f), BF),
            pltpu.VMEM((slots, 2 * f), F32),
            dma((6,)),
        ],
        flops=PRE_COST,
    )
    row_grad, to_own, to_right, to_left, to_far = call(
        middle_kernel,
        [(row_block, BF)] + [block] * 4,
        (x, rows, acc, own, right, left, far),
        [
            pltpu.VMEM((slots, width), BF),
            pltpu.VMEM((experts, capacity, width), BF),
            pltpu.VMEM((slots, 2 * f), F32),
            pltpu.VMEM((width, 2 * f), BF),
            pltpu.VMEM((width, f), BF),
            pltpu.VMEM((slots, width), BF),
            pltpu.VMEM((slots, width + EXTRA), BF),
            pltpu.VMEM(row_block, BF),
            pltpu.VMEM((4, 3 * n, f), BF),
            dma((20,)),
        ],
        mib=60,
    )
    from_far = shift(to_far, 2)
    back = lax.all_to_all(row_grad, "expert", split_axis=0, concat_axis=0, tiled=True)
    from_left = shift(to_right, 1)
    from_right = shift(to_left, -1)
    (total,) = call(
        first_sum_kernel,
        [((3 * n, f), F32)],
        (to_own, from_far),
        [pltpu.VMEM((2, 3 * n, f), BF), pltpu.VMEM((3 * n, f), F32), dma((2,))],
        flops=SUM_COST,
        mib=30,
    )
    grads = call(
        last_sum_kernel,
        [((n, f), BF)] * 3,
        (total, from_left, from_right),
        [
            pltpu.VMEM((3 * n, f), F32),
            pltpu.VMEM((2, 3 * n, f), BF),
            pltpu.VMEM((3 * n, f), BF),
            dma((12,)),
        ],
        mib=30,
    )
    token_grad, prob_t = call(
        combine_kernel,
        [((toks, width), BF), (probs_t.shape, F32)],
        (routes_t, probs_t, back),
        where=pltpu.VMEM,
        mib=16,
    )
    return (token_grad, prob_t.T, grads[0][None], grads[1][None], grads[2][None])


def solution(mesh):
    return jax.shard_map(
        shards,
        mesh=mesh,
        in_specs=(
            P(("dp", "expert"), None),
            P(("dp", "expert"), None),
            P(("dp", "expert"), None),
            P("dp", "expert", None, None),
            P("expert", "dp", None),
            P("expert", "dp", None),
            P("expert", "dp", None),
        ),
        out_specs=(
            P(("dp", "expert"), None),
            P(("dp", "expert"), None),
            P("expert", "dp", None),
            P("expert", "dp", None),
            P("expert", "dp", None),
        ),
        check_vma=False,
    )
```

time: 121 us -> 109 us (0.901)
  local copies, waits for them, and re-layouts: 14.2 us -> 3.08 us
  starting transfers between devices: 58 us -> 52.3 us
  Pallas kernels: 12.5 us -> 17.3 us
    unnamed x44 -> x14, local copies, waits for them, and re-layouts: 13.1 us -> 3.08 us
    ppermute x8 -> x6, starting transfers between devices: 27.1 us -> 21.1 us  [shift(): return lax.ppermute(value, 'dp', [(i, (i + by) % 4) for i in range(4)])]
    pallas_call x8 -> x7, Pallas kernels: 12.5 us -> 17.3 us  [call(): pl.pallas_call(body, out_shape=[jax.ShapeDtypeStruct(s, d) for s, d in ou...]
    ppermute x8 -> x6, waiting for transfers between devices: 32 us -> 35 us  [shift(): return lax.ppermute(value, 'dp', [(i, (i + by) % 4) for i in range(4)])]
    all_to_all x1, waiting for transfers between devices: 2.74 us -> 0.01 us  [shards(): lax.all_to_all(send, 'expert', split_axis=0, concat_axis=0, tiled=True)]
  transfers between devices with their start and end apart: 10 -> 8, of which waited for: 5 -> 4; matrix products, arithmetic and copies ran while one was open for 1% -> 0% of each run, Pallas kernels for 6% -> 7%
where the time goes in v2:
time: 109 us; the launch traced here: 108 us
  starting transfers between devices  52.3 us (48%)
  waiting for transfers between devices  35 us (32%)
  Pallas kernels  17.3 us (16%)
  local copies, waits for them, and re-layouts  3.08 us (3%)
    ppermute x6, waiting for transfers between devices, shift(): return lax.ppermute(value, 'dp', [(i, (i + by) % 4) for i in range(4)])  35 us
    ppermute x6, starting transfers between devices, shift(): return lax.ppermute(value, 'dp', [(i, (i + by) % 4) for i in range(4)])  21.1 us
    all_to_all x1, starting transfers between devices, shards(): lax.all_to_all(send, 'expert', split_axis=0, concat_axis=0, tiled=True)  17.4 us
    pallas_call x7, Pallas kernels, call(): pl.pallas_call(body, out_shape=[jax.ShapeDtypeStruct(s, d) for s, d in ou...  17.3 us
    all_to_all x1, starting transfers between devices, shards(): lax.all_to_all(row_grad, 'expert', split_axis=0, concat_axis=0, tiled=True)  13.7 us
    unnamed x14, local copies, waits for them, and re-layouts  3.08 us
  transfers between devices with their start and end apart: 8, of which 4 were waited for; matrix products, arithmetic and copies ran while one was open for 0% of the time, Pallas kernels for 7%

profile of v2, /device:TPU:14, one launch (start us, length us, event | category | flops | bytes accessed | tf_op | source)
XLA Modules:
  0.0 108.4 jit_solution(6182384124433629050)
XLA Ops:
  0.7 1.9 %shard_map.111.own = bf16[1152,384]{1,0:T(8,128)(2,1)} custom-call(bf16[384,384]{1,0:T(8,128)(2,1)} %bitcast.16, bf16[384,384]{1,0:T(8,128)(2,1)} %bitcast.17, bf16[384,384]{1,0:T(8,128)(2,1)} %bitcast.18), custom_call_target="tpu_custom_call" | custom-call | tf_op jit(solution)/shard_map/pallas_call | solution.py:30
  2.6 3.4 %collective-permute-start = (bf16[1152,384]{1,0:T(8,128)(2,1)}, bf16[1152,384]{1,0:T(8,128)(2,1)S(1)}, u32[]{:S(2)}, u32[]{:S(2)}) collective-permute-start(bf16[1152,384]{1,0:T(8,128)(2,1)} %shard_map.111.own), channel_id=1, source_target_pairs={{0,256},{128,384},{256,0},{384,128},{1,257},{129,385},{257,1},{385... | collective-permute-start | bytes 2654216 | tf_op jit(solution)/shard_map/ppermute | solution.py:202
  6.1 1.6 %shard_map.110 = bf16[128,2,1536]{2,1,0:T(2,128)(2,1)} custom-call(s32[8,16]{1,0:T(8,128)S(1)} %bitcast.10, f32[8,16]{1,0:T(8,128)S(1)} %bitcast.12, bf16[16,1536]{1,0:T(8,128)(2,1)S(1)} %copy-done), custom_call_target="tpu_custom_call" | custom-call | tf_op jit(solution)/shard_map/pallas_call | solution.py:30
  7.7 17.4 %all-to-all-start = ((bf16[128,2,1536]{2,1,0:T(2,128)(2,1)}), bf16[128,2,1536]{2,1,0:T(2,128)(2,1)S(1)}, u32[]{:S(2)}, u32[]{:S(2)}) async-start(bf16[128,2,1536]{2,1,0:T(2,128)(2,1)} %shard_map.110), calls=%async_computation | async-start | bytes 1572864 | tf_op jit(solution)/shard_map/all_to_all | solution.py:228
  25.1 1.9 %collective-permute-start.2 = (bf16[1152,384]{1,0:T(8,128)(2,1)S(1)}, bf16[1152,384]{1,0:T(8,128)(2,1)}, u32[]{:S(2)}, u32[]{:S(2)}) collective-permute-start(bf16[1152,384]{1,0:T(8,128)(2,1)S(1)} %copy-done.4), channel_id=1, source_target_pairs={{0,384},{128,0},{256,128},{384,256},{1,385},{129,1},{257,129},{385... | collective-permute-start | bytes 2654216 | tf_op jit(solution)/shard_map/ppermute | solution.py:202
  27.0 5.1 %collective-permute-start.1 = (bf16[1152,384]{1,0:T(8,128)(2,1)S(1)}, bf16[1152,384]{1,0:T(8,128)(2,1)}, u32[]{:S(2)}, u32[]{:S(2)}) collective-permute-start(bf16[1152,384]{1,0:T(8,128)(2,1)S(1)} %copy-done.4), channel_id=1, source_target_pairs={{0,128},{128,256},{256,384},{384,0},{1,129},{129,257},{257,385},{3... | collective-permute-start | bytes 2654216 | tf_op jit(solution)/shard_map/ppermute | solution.py:202
  32.2 0.0 collective-permute-done.far
  32.2 1.0 copy-done.6
  33.2 2.9 %shard_map.112.acc_hbm = f32[256,768]{1,0:T(8,128)} custom-call(bf16[256,1536]{1,0:T(8,128)(2,1)} %bitcast.14, bf16[1152,384]{1,0:T(8,128)(2,1)} %shard_map.111.own, bf16[1152,384]{1,0:T(8,128)(2,1)} %copy-done.6), custom_call_target="tpu_custom_call" | custom-call | flops 12582912000 | tf_op jit(solution)/shard_map/pallas_call | solution.py:30
  36.1 14.0 %collective-permute-done.2.left = bf16[1152,384]{1,0:T(8,128)(2,1)} collective-permute-done((bf16[1152,384]{1,0:T(8,128)(2,1)S(1)}, bf16[1152,384]{1,0:T(8,128)(2,1)}, u32[]{:S(2)}, u32[]{:S(2)}) %collective-permute-start.2) | collective-permute-done | bytes 884768 | tf_op jit(solution)/shard_map/ppermute | solution.py:202
  50.0 1.1 collective-permute-done.1.right
  51.1 0.0 all-to-all-done.rows_hbm
  51.1 0.9 copy-done.5
  52.0 6.9 %shard_map.113 = (bf16[128,2,1664]{2,1,0:T(2,128)(2,1)}, bf16[1152,384]{1,0:T(8,128)(2,1)}, bf16[1152,384]{1,0:T(8,128)(2,1)}, bf16[1152,384]{1,0:T(8,128)(2,1)}, bf16[1152,384]{1,0:T(8,128)(2,1)}) custom-call(bf16[256,1536]{1,0:T(8,128)(2,1)} %bitcast.15, bf16[128,2,1536]{2,1,0:T(2,128)(2,1)} %copy-done.5, f32[256,768]{1,0:T(8,128)} %shard_map.112.acc_hbm, ...), custom_call_target="tpu_custom_call" | custom-call | tf_op jit(solution)/shard_map/pallas_call | solution.py:30
  58.9 4.8 %collective-permute-start.3 = (bf16[1152,384]{1,0:T(8,128)(2,1)}, bf16[1152,384]{1,0:T(8,128)(2,1)S(1)}, u32[]{:S(2)}, u32[]{:S(2)}) collective-permute-start(bf16[1152,384]{1,0:T(8,128)(2,1)} %get-tuple-element.19), channel_id=1, source_target_pairs={{0,256},{128,384},{256,0},{384,128},{1,257},{129,385},{257,1},{385... | collective-permute-start | bytes 2654216 | tf_op jit(solution)/shard_map/ppermute | solution.py:202
  63.7 13.7 %all-to-all-start.1 = ((bf16[128,2,1664]{2,1,0:T(2,128)(2,1)}), bf16[128,2,1664]{2,1,0:T(2,128)(2,1)S(1)}, u32[]{:S(2)}, u32[]{:S(2)}) async-start(bf16[128,2,1664]{2,1,0:T(2,128)(2,1)} %get-tuple-element.15), calls=%async_computation.1 | async-start | bytes 1703936 | tf_op jit(solution)/shard_map/all_to_all | solution.py:262
  77.5 3.1 %collective-permute-start.4 = (bf16[1152,384]{1,0:T(8,128)(2,1)}, bf16[1152,384]{1,0:T(8,128)(2,1)S(1)}, u32[]{:S(2)}, u32[]{:S(2)}) collective-permute-start(bf16[1152,384]{1,0:T(8,128)(2,1)} %get-tuple-element.20), channel_id=1, source_target_pairs={{0,128},{128,256},{256,384},{384,0},{1,129},{129,257},{257,385},{3... | collective-permute-start | bytes 2654216 | tf_op jit(solution)/shard_map/ppermute | solution.py:202
  80.6 2.7 %collective-permute-start.5 = (bf16[1152,384]{1,0:T(8,128)(2,1)}, bf16[1152,384]{1,0:T(8,128)(2,1)S(1)}, u32[]{:S(2)}, u32[]{:S(2)}) collective-permute-start(bf16[1152,384]{1,0:T(8,128)(2,1)} %get-tuple-element.21), channel_id=1, source_target_pairs={{0,384},{128,0},{256,128},{384,256},{1,385},{129,1},{257,129},{385... | collective-permute-start | bytes 2654216 | tf_op jit(solution)/shard_map/ppermute | solution.py:202
  83.4 1.2 %copy-done.3 = bf16[1152,384]{1,0:T(8,128)(2,1)S(1)} copy-done((bf16[1152,384]{1,0:T(8,128)(2,1)S(1)}, bf16[1152,384]{1,0:T(8,128)(2,1)}, u32[]{:S(2)}) %copy-start.3) | copy-done | bytes 884760
  84.5 0.9 shard_map.115.sum_hbm
  85.5 17.7 %collective-permute-done.4.a = bf16[1152,384]{1,0:T(8,128)(2,1)S(1)} collective-permute-done((bf16[1152,384]{1,0:T(8,128)(2,1)}, bf16[1152,384]{1,0:T(8,128)(2,1)S(1)}, u32[]{:S(2)}, u32[]{:S(2)}) %collective-permute-start.4) | collective-permute-done | bytes 884768 | tf_op jit(solution)/shard_map/ppermute | solution.py:202
  103.2 2.2 %collective-permute-done.5.b = bf16[1152,384]{1,0:T(8,128)(2,1)S(1)} collective-permute-done((bf16[1152,384]{1,0:T(8,128)(2,1)}, bf16[1152,384]{1,0:T(8,128)(2,1)S(1)}, u32[]{:S(2)}, u32[]{:S(2)}) %collective-permute-start.5) | collective-permute-done | bytes 884768 | tf_op jit(solution)/shard_map/ppermute | solution.py:202
  105.4 1.8 %shard_map.116 = (bf16[384,384]{1,0:T(8,128)(2,1)}, bf16[384,384]{1,0:T(8,128)(2,1)}, bf16[384,384]{1,0:T(8,128)(2,1)}) custom-call(f32[1152,384]{1,0:T(8,128)S(1)} %shard_map.115.sum_hbm, bf16[1152,384]{1,0:T(8,128)(2,1)S(1)} %collective-permute-done.4.a, bf16[1152,384]{1,0:T(8,128)(2,1)S(1)} %collective-permute-done.5.b), custom_call_target="tpu_custom_call" | custom-call | tf_op jit(solution)/shard_map/pallas_call | solution.py:30
  107.2 1.2 %shard_map.114 = (bf16[16,1536]{1,0:T(8,128)(2,1)}, f32[8,16]{1,0:T(8,128)}) custom-call(s32[8,16]{1,0:T(8,128)S(1)} %bitcast.11, f32[8,16]{1,0:T(8,128)S(1)} %bitcast.13, bf16[128,2,1664]{2,1,0:T(2,128)(2,1)S(1)} %all-to-all-done.1.back_ref), custom_call_target="tpu_custom_call" | custom-call | tf_op jit(solution)/shard_map/pallas_call | solution.py:30
  (13 shorter events, 0.0 us)
Async XLA Ops:
  0.6 5.4 %copy-start.2 = (f32[16,8]{0,1:T(8,128)S(1)}, f32[16,8]{0,1:T(8,128)}, u32[]{:S(2)}) copy-start(f32[16,8]{0,1:T(8,128)} %param.9) | copy-start | bytes 1540
  0.6 5.4 %copy-start.1 = (s32[16,8]{0,1:T(8,128)S(1)}, s32[16,8]{0,1:T(8,128)}, u32[]{:S(2)}) copy-start(s32[16,8]{0,1:T(8,128)} %param.8) | copy-start | bytes 1540
  0.7 5.4 %copy-start = (bf16[16,1536]{1,0:T(8,128)(2,1)S(1)}, bf16[16,1536]{1,0:T(8,128)(2,1)}, u32[]{:S(2)}) copy-start(bf16[16,1536]{1,0:T(8,128)(2,1)} %grad_ref.1) | copy-start | bytes 147460
  2.6 22.5 %copy-start.4 = (bf16[1152,384]{1,0:T(8,128)(2,1)S(1)}, bf16[1152,384]{1,0:T(8,128)(2,1)}, u32[]{:S(2)}) copy-start(bf16[1152,384]{1,0:T(8,128)(2,1)} %shard_map.111.own) | copy-start | bytes 2654212
  2.6 29.6 %collective-permute-start = (bf16[1152,384]{1,0:T(8,128)(2,1)}, bf16[1152,384]{1,0:T(8,128)(2,1)S(1)}, u32[]{:S(2)}, u32[]{:S(2)}) collective-permute-start(bf16[1152,384]{1,0:T(8,128)(2,1)} %shard_map.111.own), channel_id=1, source_target_pairs={{0,256},{128,384},{256,0},{384,128},{1,257},{129,385},{257,1},{385... | collective-permute-start | bytes 2654216 | tf_op jit(solution)/shard_map/ppermute | solution.py:202
  7.7 43.4 %all-to-all-start = ((bf16[128,2,1536]{2,1,0:T(2,128)(2,1)}), bf16[128,2,1536]{2,1,0:T(2,128)(2,1)S(1)}, u32[]{:S(2)}, u32[]{:S(2)}) async-start(bf16[128,2,1536]{2,1,0:T(2,128)(2,1)} %shard_map.110), calls=%async_computation | async-start | bytes 1572864 | tf_op jit(solution)/shard_map/all_to_all | solution.py:228
  25.1 24.9 %collective-permute-start.2 = (bf16[1152,384]{1,0:T(8,128)(2,1)S(1)}, bf16[1152,384]{1,0:T(8,128)(2,1)}, u32[]{:S(2)}, u32[]{:S(2)}) collective-permute-start(bf16[1152,384]{1,0:T(8,128)(2,1)S(1)} %copy-done.4), channel_id=1, source_target_pairs={{0,384},{128,0},{256,128},{384,256},{1,385},{129,1},{257,129},{385... | collective-permute-start | bytes 2654216 | tf_op jit(solution)/shard_map/ppermute | solution.py:202
  27.0 24.1 %collective-permute-start.1 = (bf16[1152,384]{1,0:T(8,128)(2,1)S(1)}, bf16[1152,384]{1,0:T(8,128)(2,1)}, u32[]{:S(2)}, u32[]{:S(2)}) collective-permute-start(bf16[1152,384]{1,0:T(8,128)(2,1)S(1)} %copy-done.4), channel_id=1, source_target_pairs={{0,128},{128,256},{256,384},{384,0},{1,129},{129,257},{257,385},{3... | collective-permute-start | bytes 2654216 | tf_op jit(solution)/shard_map/ppermute | solution.py:202
  32.2 1.0 copy-start.6
  51.1 0.9 copy-start.5
  58.9 24.4 %collective-permute-start.3 = (bf16[1152,384]{1,0:T(8,128)(2,1)}, bf16[1152,384]{1,0:T(8,128)(2,1)S(1)}, u32[]{:S(2)}, u32[]{:S(2)}) collective-permute-start(bf16[1152,384]{1,0:T(8,128)(2,1)} %get-tuple-element.19), channel_id=1, source_target_pairs={{0,256},{128,384},{256,0},{384,128},{1,257},{129,385},{257,1},{385... | collective-permute-start | bytes 2654216 | tf_op jit(solution)/shard_map/ppermute | solution.py:202
  63.7 43.5 %all-to-all-start.1 = ((bf16[128,2,1664]{2,1,0:T(2,128)(2,1)}), bf16[128,2,1664]{2,1,0:T(2,128)(2,1)S(1)}, u32[]{:S(2)}, u32[]{:S(2)}) async-start(bf16[128,2,1664]{2,1,0:T(2,128)(2,1)} %get-tuple-element.15), calls=%async_computation.1 | async-start | bytes 1703936 | tf_op jit(solution)/shard_map/all_to_all | solution.py:262
  77.5 25.7 %collective-permute-start.4 = (bf16[1152,384]{1,0:T(8,128)(2,1)}, bf16[1152,384]{1,0:T(8,128)(2,1)S(1)}, u32[]{:S(2)}, u32[]{:S(2)}) collective-permute-start(bf16[1152,384]{1,0:T(8,128)(2,1)} %get-tuple-element.20), channel_id=1, source_target_pairs={{0,128},{128,256},{256,384},{384,0},{1,129},{129,257},{257,385},{3... | collective-permute-start | bytes 2654216 | tf_op jit(solution)/shard_map/ppermute | solution.py:202
  80.6 24.7 %collective-permute-start.5 = (bf16[1152,384]{1,0:T(8,128)(2,1)}, bf16[1152,384]{1,0:T(8,128)(2,1)S(1)}, u32[]{:S(2)}, u32[]{:S(2)}) collective-permute-start(bf16[1152,384]{1,0:T(8,128)(2,1)} %get-tuple-element.21), channel_id=1, source_target_pairs={{0,384},{128,0},{256,128},{384,256},{1,385},{129,1},{257,129},{385... | collective-permute-start | bytes 2654216 | tf_op jit(solution)/shard_map/ppermute | solution.py:202
  83.4 1.2 %copy-start.3 = (bf16[1152,384]{1,0:T(8,128)(2,1)S(1)}, bf16[1152,384]{1,0:T(8,128)(2,1)}, u32[]{:S(2)}) copy-start(bf16[1152,384]{1,0:T(8,128)(2,1)} %get-tuple-element.18.own) | copy-start | bytes 2654212

commit v3 on v2

--- a/solution.py
+++ b/solution.py
@@ -11,6 +11,8 @@
 F32 = jnp.float32
 PRE_COST = 12000 << 20
 SUM_COST = 12000 << 20
+MID_MIB = 52
+LAST_MIB = 20
 
 
 def dot(a, b):
@@ -26,12 +28,13 @@
 
 
 def call(body, outs, args, scratch=(), flops=0, where=pltpu.HBM, mib=61):
-    spec = pl.BlockSpec(memory_space=where)
+    spaces = where if isinstance(where, tuple) else (where,) * (len(args) + len(outs))
+    specs = [pl.BlockSpec(memory_space=space) for space in spaces]
     return pl.pallas_call(
         body,
         out_shape=[jax.ShapeDtypeStruct(s, d) for s, d in outs],
-        in_specs=[spec] * len(args),
-        out_specs=[spec] * len(outs),
+        in_specs=specs[: len(args)],
+        out_specs=specs[len(args) :],
         scratch_shapes=list(scratch),
         compiler_params=pltpu.CompilerParams(vmem_limit_bytes=mib * 1024 * 1024),
         cost_estimate=pl.CostEstimate(flops=flops, bytes_accessed=0, transcendentals=0),
@@ -65,10 +68,40 @@
     return mine, hits
 
 
-def build_kernel(routes_ref, probs_ref, grad_ref, out_ref):
-    experts, capacity, width = out_ref.shape
-    slots = experts * capacity
+def combine_kernel(routes_ref, probs_ref, back_ref, token_ref, prob_ref):
+    experts, capacity, wide = back_ref.shape
+    slots, width = experts * capacity, token_ref.shape[1]
     mine, hits = places(routes_ref[...], slots, capacity)
+    picks = mine.astype(BF)
+    n = width // 4
+    for i in range(4):
+        cols = slice(i * n, (i + 1) * n)
+        token_ref[:, cols] = dot_tn(picks, back_ref[:, :, cols].reshape(slots, n)).astype(BF)
+    extra = back_ref[:, :, width:].reshape(slots, wide - width)
+    value = jnp.sum(extra.astype(F32), axis=1, keepdims=True)
+    probs = probs_ref[...]
+    for k, hit in enumerate(hits):
+        got = jnp.sum(jnp.where(hit & mine, value, 0.0), axis=0, keepdims=True)
+        prob_ref[k : k + 1, :] = got / probs[k : k + 1, :]
+
+
+def open_kernel(
+    a_hbm, b_hbm, c_hbm, routes_hbm, probs_hbm, grad_hbm, own_hbm, send_hbm,
+    own_ref, routes_ref, probs_ref, grad_ref, send_ref, sems,
+):
+    n = a_hbm.shape[0]
+    experts, capacity, width = send_ref.shape
+    shard = start(
+        [(r, own_ref.at[pl.ds(i * n, n), :]) for i, r in enumerate((a_hbm, b_hbm, c_hbm))], sems
+    )
+    small = start(
+        [(routes_hbm, routes_ref), (probs_hbm, probs_ref), (grad_hbm, grad_ref)],
+        sems.at[pl.ds(3, 3)],
+    )
+    finish(shard)
+    out = start([(own_ref, own_hbm)], sems.at[pl.ds(6, 1)])
+    finish(small)
+    mine, hits = places(routes_ref[...], experts * capacity, capacity)
     probs = probs_ref[...]
     weight = jnp.zeros(mine.shape, F32)
     for k, hit in enumerate(hits):
@@ -76,33 +109,11 @@
     weight = jnp.where(mine, weight, 0.0)
     high = weight.astype(BF)
     low = (weight - high.astype(F32)).astype(BF)
-    grad = grad_ref[...]
-    rows = (dot(high, grad) + dot(low, grad)).astype(BF)
-    out_ref[...] = rows.reshape(experts, capacity, width)
-
-
-def combine_kernel(routes_ref, probs_ref, back_ref, token_ref, prob_ref):
-    experts, capacity, wide = back_ref.shape
-    slots, width = experts * capacity, token_ref.shape[1]
-    back = back_ref[...].reshape(slots, wide)
-    mine, hits = places(routes_ref[...], slots, capacity)
-    token_ref[...] = dot_tn(mine.astype(BF), back[:, :width]).astype(BF)
-    value = jnp.sum(back[:, width:].astype(F32), axis=1, keepdims=True)
-    probs = probs_ref[...]
-    for k, hit in enumerate(hits):
-        got = jnp.sum(jnp.where(hit & mine, value, 0.0), axis=0, keepdims=True)
-        prob_ref[k : k + 1, :] = got / probs[k : k + 1, :]
-
-
-def pack_kernel(a_ref, b_ref, c_ref, out_hbm, out_ref, sems):
-    n = a_ref.shape[0]
-    blocks = [pl.ds(i * n, n) for i in range(3)]
-    copies = start([(r, out_ref.at[at, :]) for r, at in zip((a_ref, b_ref, c_ref), blocks)], sems)
-    out = []
-    for i, at in enumerate(blocks):
-        copies[i].wait()
-        out += start([(out_ref.at[at, :], out_hbm.at[at, :])], sems.at[pl.ds(3 + i, 1)])
-    finish(out)
+    for i in range(4):
+        cols = slice(i * n, (i + 1) * n)
+        rows = dot(high, grad_ref[:, cols]) + dot(low, grad_ref[:, cols])
+        send_ref[:, :, cols] = rows.astype(BF).reshape(experts, capacity, n)
+    finish(out + start([(send_ref, send_hbm)], sems.at[pl.ds(7, 1)]))
 
 
 def span(offset, n):
@@ -124,25 +135,30 @@
 
 
 def middle_kernel(
-    x_hbm, rows_hbm, acc_hbm, own, right, left, far,
+    x_ref, rows_ref, acc_hbm, own, right, left, far,
     back_hbm, to_own, to_right, to_left, to_far,
-    x_ref, rows_ref, acc_ref, w_ref, wd_ref, g_ref, row_ref, back_ref, part_ref, sems,
+    acc_ref, w_ref, wd_ref, g_ref, back_ref, part_ref, sems,
 ):
     width, n, f = x_ref.shape[1], x_ref.shape[1] // 4, wd_ref.shape[1]
-    moves = [(rows_hbm, rows_ref), (x_hbm, x_ref), (acc_hbm, acc_ref)]
-    for offset, block in ((3, right), (1, left), (0, own), (2, far)):
-        at = span(offset, n)
-        moves.append((block.at[pl.ds(0, n), :], w_ref.at[at, pl.ds(0, f)]))
-        moves.append((block.at[pl.ds(n, n), :], w_ref.at[at, pl.ds(f, f)]))
-        moves.append((block.at[pl.ds(2 * n, n), :], wd_ref.at[at, :]))
+    blocks = ((3, right), (1, left), (0, own), (2, far))
+    moves = [(b.at[pl.ds(2 * n, n), :], wd_ref.at[span(i, n), :]) for i, b in blocks]
+    moves += [(acc_hbm, acc_ref)]
+    for i, b in blocks:
+        moves += [(b.at[pl.ds(k * n, n), :], w_ref.at[span(i, n), pl.ds(k * f, f)]) for k in (0, 1)]
     copies = start(moves, sems)
-    finish(copies[0:1])
-    g_ref[...] = rows_ref[...].reshape(g_ref.shape)
-    finish(copies[1:])
+    slots, shape = x_ref.shape[0], rows_ref.shape
+    finish(copies[0:4])
+    dh = None
+    for i in range(4):
+        cols = slice(i * n, (i + 1) * n)
+        rows = rows_ref[:, :, cols].reshape(slots, n)
+        g_ref[:, cols] = rows
+        term = dot(rows, wd_ref[cols, :])
+        dh = term if dh is None else dh + term
+    finish(copies[4:9])
     pre = acc_ref[...]
     for offset in (3, 1):
         pre = pre + dot(x_ref[:, span(offset, n)], w_ref[span(offset, n), :])
-    dh = dot(g_ref[...], wd_ref[...])
     gate, up = pre[:, :f], pre[:, f:]
     sig = jax.nn.sigmoid(gate)
     act = gate * sig
@@ -160,15 +176,14 @@
         part_ref[k, n : 2 * n, :] = part[:, f:]
         part_ref[k, 2 * n :, :] = dot_tn(g_ref[:, cols], hidden).astype(BF)
         out += start([(part_ref.at[k], to)], sems.at[pl.ds(15 + k, 1)])
+    finish(copies[9:13])
     for i in range(4):
         at = slice(i * n, (i + 1) * n)
-        row_ref[:, at] = dot_nt(both, w_ref[at, :]).astype(BF)
+        back_ref[:, :, at] = dot_nt(both, w_ref[at, :]).astype(BF).reshape(*shape[:2], n)
     lane = lax.broadcasted_iota(jnp.int32, (x_ref.shape[0], EXTRA), 1)
     high = row_prob.astype(BF).astype(F32)
-    row_ref[:, width:] = jnp.where(
-        lane == 0, high, jnp.where(lane == 1, row_prob - high, 0.0)
-    ).astype(BF)
-    back_ref[...] = row_ref[...].reshape(back_ref.shape)
+    extra = jnp.where(lane == 0, high, jnp.where(lane == 1, row_prob - high, 0.0)).astype(BF)
+    back_ref[:, :, width:] = extra.reshape(*shape[:2], EXTRA)
     out += start([(back_ref, back_hbm)], sems.at[pl.ds(19, 1)])
     finish(out)
 
@@ -179,22 +194,15 @@
     finish(start([(sum_ref, sum_hbm)], sems))
 
 
-def last_sum_kernel(sum_hbm, a, b, gate_hbm, up_hbm, down_hbm, sum_ref, in_ref, out_ref, sems):
+def last_sum_kernel(sum_ref, a_ref, b_ref, gate_hbm, up_hbm, down_hbm, out_ref, sems):
     n = gate_hbm.shape[0]
-    blocks = [pl.ds(i * n, n) for i in range(3)]
-    moves = []
-    for at in blocks:
-        moves += [(sum_hbm.at[at, :], sum_ref.at[at, :])]
-        moves += [(r.at[at, :], in_ref.at[k, at, :]) for k, r in enumerate((a, b))]
-    copies = start(moves, sems)
     out = []
     for i, hbm in enumerate((gate_hbm, up_hbm, down_hbm)):
-        finish(copies[3 * i : 3 * i + 3])
-        at = blocks[i]
+        at = pl.ds(i * n, n)
         out_ref[at, :] = (
-            sum_ref[at, :] + in_ref[0, at, :].astype(F32) + in_ref[1, at, :].astype(F32)
+            sum_ref[at, :] + a_ref[at, :].astype(F32) + b_ref[at, :].astype(F32)
         ).astype(BF)
-        out += start([(out_ref.at[at, :], hbm)], sems.at[pl.ds(9 + i, 1)])
+        out += start([(out_ref.at[at, :], hbm)], sems.at[pl.ds(i, 1)])
     finish(out)
 
 
@@ -214,17 +222,20 @@
     block = ((3 * n, f), BF)
     row_block = (experts, capacity, width + EXTRA)
 
-    (own,) = call(
-        pack_kernel, [block], (w_gate[0], w_up[0], w_down[0]), [pltpu.VMEM(*block), dma((6,))]
+    own, send = call(
+        open_kernel,
+        [block, ((experts, capacity, width), BF)],
+        (w_gate[0], w_up[0], w_down[0], routes_t, probs_t, out_grad),
+        [
+            pltpu.VMEM(*block),
+            pltpu.VMEM(routes_t.shape, jnp.int32),
+            pltpu.VMEM(probs_t.shape, F32),
+            pltpu.VMEM(out_grad.shape, BF),
+            pltpu.VMEM((experts, capacity, width), BF),
+            dma((8,)),
+        ],
     )
     far = shift(own, 2)
-    (send,) = call(
-        build_kernel,
-        [((experts, capacity, width), BF)],
-        (routes_t, probs_t, out_grad),
-        where=pltpu.VMEM,
-        mib=16,
-    )
     rows = lax.all_to_all(send, "expert", split_axis=0, concat_axis=0, tiled=True)
     right = shift(own, 1)
     left = shift(own, -1)
@@ -245,18 +256,16 @@
         [(row_block, BF)] + [block] * 4,
         (x, rows, acc, own, right, left, far),
         [
-            pltpu.VMEM((slots, width), BF),
-            pltpu.VMEM((experts, capacity, width), BF),
             pltpu.VMEM((slots, 2 * f), F32),
             pltpu.VMEM((width, 2 * f), BF),
             pltpu.VMEM((width, f), BF),
             pltpu.VMEM((slots, width), BF),
-            pltpu.VMEM((slots, width + EXTRA), BF),
             pltpu.VMEM(row_block, BF),
             pltpu.VMEM((4, 3 * n, f), BF),
             dma((20,)),
         ],
-        mib=60,
+        where=(pltpu.VMEM,) * 2 + (pltpu.HBM,) * 10,
+        mib=MID_MIB,
     )
     from_far = shift(to_far, 2)
     back = lax.all_to_all(row_grad, "expert", split_axis=0, concat_axis=0, tiled=True)
@@ -274,13 +283,9 @@
         last_sum_kernel,
         [((n, f), BF)] * 3,
         (total, from_left, from_right),
-        [
-            pltpu.VMEM((3 * n, f), F32),
-            pltpu.VMEM((2, 3 * n, f), BF),
-            pltpu.VMEM((3 * n, f), BF),
-            dma((12,)),
-        ],
-        mib=30,
+        [pltpu.VMEM((3 * n, f), BF), dma((3,))],
+        where=(pltpu.VMEM,) * 3 + (pltpu.HBM,) * 3,
+        mib=LAST_MIB,
     )
     token_grad, prob_t = call(
         combine_kernel,

time: 109 us -> 106 us (0.972)
  Pallas kernels: 17.3 us -> 15.2 us
    pallas_call x7 -> x6, Pallas kernels: 17.3 us -> 15.2 us  [call(): pl.pallas_call(body, out_shape=[jax.ShapeDtypeStruct(s, d) for s, d in ou...]
    unnamed x14 -> x10, local copies, waits for them, and re-layouts: 3.08 us -> 2.16 us
  transfers between devices with their start and end apart: 8 -> 8, of which waited for: 4 -> 4; matrix products, arithmetic and copies ran while one was open for 0% -> 0% of each run, Pallas kernels for 7% -> 5%
where the time goes in v3:
time: 106 us
  starting transfers between devices  52 us (49%)
  waiting for transfers between devices  35.3 us (33%)
  Pallas kernels  15.2 us (14%)
  local copies, waits for them, and re-layouts  2.16 us (2%)
    ppermute x6, waiting for transfers between devices, shift(): return lax.ppermute(value, 'dp', [(i, (i + by) % 4) for i in range(4)])  35.3 us
    ppermute x6, starting transfers between devices, shift(): return lax.ppermute(value, 'dp', [(i, (i + by) % 4) for i in range(4)])  20.9 us
    all_to_all x1, starting transfers between devices, shards(): lax.all_to_all(send, 'expert', split_axis=0, concat_axis=0, tiled=True)  17.4 us
    pallas_call x6, Pallas kernels, call(): pl.pallas_call(body, out_shape=[jax.ShapeDtypeStruct(s, d) for s, d in ou...  15.2 us
    all_to_all x1, starting transfers between devices, shards(): lax.all_to_all(row_grad, 'expert', split_axis=0, concat_axis=0, tiled=True)  13.7 us
    unnamed x10, local copies, waits for them, and re-layouts  2.16 us
  transfers between devices with their start and end apart: 8, of which 4 were waited for; matrix products, arithmetic and copies ran while one was open for 0% of the time, Pallas kernels for 5%

profile of v3, /device:TPU:14, one launch (start us, length us, event | category | flops | bytes accessed | tf_op | source)
XLA Modules:
  0.0 105.5 jit_solution(16226909169079843299)
XLA Ops:
  0.6 2.9 %shard_map.110 = (bf16[1152,384]{1,0:T(8,128)(2,1)}, bf16[128,2,1536]{2,1,0:T(2,128)(2,1)}) custom-call(bf16[384,384]{1,0:T(8,128)(2,1)} %bitcast.16, bf16[384,384]{1,0:T(8,128)(2,1)} %bitcast.17, bf16[384,384]{1,0:T(8,128)(2,1)} %bitcast.18, s32[8,16]{1,0:T(8,128)} %bitcast.12, f32[8,16]{1,0:T(8,128)} %bitcast.14, bf16[16,1536]{1,0:T(8,128)(2,1)} %grad_hbm.1), custom_call_target="tpu_custom_call" | custom-call | tf_op jit(solution)/shard_map/pallas_call | solution.py:33
  3.6 3.3 %collective-permute-start = (bf16[1152,384]{1,0:T(8,128)(2,1)}, bf16[1152,384]{1,0:T(8,128)(2,1)S(1)}, u32[]{:S(2)}, u32[]{:S(2)}) collective-permute-start(bf16[1152,384]{1,0:T(8,128)(2,1)} %get-tuple-element.18.own), channel_id=1, source_target_pairs={{0,256},{128,384},{256,0},{384,128},{1,257},{129,385},{257,1},{385... | collective-permute-start | bytes 2654216 | tf_op jit(solution)/shard_map/ppermute | solution.py:210
  6.9 17.4 %all-to-all-start = ((bf16[128,2,1536]{2,1,0:T(2,128)(2,1)}), bf16[128,2,1536]{2,1,0:T(2,128)(2,1)S(1)}, u32[]{:S(2)}, u32[]{:S(2)}) async-start(bf16[128,2,1536]{2,1,0:T(2,128)(2,1)} %get-tuple-element.17), calls=%async_computation | async-start | bytes 1572864 | tf_op jit(solution)/shard_map/all_to_all | solution.py:239
  24.3 1.9 %collective-permute-start.2 = (bf16[1152,384]{1,0:T(8,128)(2,1)}, bf16[1152,384]{1,0:T(8,128)(2,1)}, u32[]{:S(2)}, u32[]{:S(2)}) collective-permute-start(bf16[1152,384]{1,0:T(8,128)(2,1)} %get-tuple-element.18.own), channel_id=1, source_target_pairs={{0,384},{128,0},{256,128},{384,256},{1,385},{129,1},{257,129},{385... | collective-permute-start | bytes 2654216 | tf_op jit(solution)/shard_map/ppermute | solution.py:210
  26.2 5.1 %collective-permute-start.1 = (bf16[1152,384]{1,0:T(8,128)(2,1)}, bf16[1152,384]{1,0:T(8,128)(2,1)}, u32[]{:S(2)}, u32[]{:S(2)}) collective-permute-start(bf16[1152,384]{1,0:T(8,128)(2,1)} %get-tuple-element.18.own), channel_id=1, source_target_pairs={{0,128},{128,256},{256,384},{384,0},{1,129},{129,257},{257,385},{3... | collective-permute-start | bytes 2654216 | tf_op jit(solution)/shard_map/ppermute | solution.py:210
  31.4 0.0 collective-permute-done.far
  31.4 1.0 copy-done.4
  32.4 2.9 %shard_map.111.acc_hbm = f32[256,768]{1,0:T(8,128)} custom-call(bf16[256,1536]{1,0:T(8,128)(2,1)} %bitcast.10, bf16[1152,384]{1,0:T(8,128)(2,1)} %get-tuple-element.18.own, bf16[1152,384]{1,0:T(8,128)(2,1)} %copy-done.4), custom_call_target="tpu_custom_call" | custom-call | flops 12582912000 | tf_op jit(solution)/shard_map/pallas_call | solution.py:33
  35.3 14.1 %collective-permute-done.2.left = bf16[1152,384]{1,0:T(8,128)(2,1)} collective-permute-done((bf16[1152,384]{1,0:T(8,128)(2,1)}, bf16[1152,384]{1,0:T(8,128)(2,1)}, u32[]{:S(2)}, u32[]{:S(2)}) %collective-permute-start.2) | collective-permute-done | bytes 884768 | tf_op jit(solution)/shard_map/ppermute | solution.py:210
  49.4 1.2 %collective-permute-done.1.right = bf16[1152,384]{1,0:T(8,128)(2,1)} collective-permute-done((bf16[1152,384]{1,0:T(8,128)(2,1)}, bf16[1152,384]{1,0:T(8,128)(2,1)}, u32[]{:S(2)}, u32[]{:S(2)}) %collective-permute-start.1) | collective-permute-done | bytes 884768 | tf_op jit(solution)/shard_map/ppermute | solution.py:210
  50.6 0.0 all-to-all-done.rows_ref
  50.6 6.1 %shard_map.112 = (bf16[128,2,1664]{2,1,0:T(2,128)(2,1)}, bf16[1152,384]{1,0:T(8,128)(2,1)}, bf16[1152,384]{1,0:T(8,128)(2,1)}, bf16[1152,384]{1,0:T(8,128)(2,1)}, bf16[1152,384]{1,0:T(8,128)(2,1)}) custom-call(bf16[256,1536]{1,0:T(8,128)(2,1)S(1)} %bitcast.11, bf16[128,2,1536]{2,1,0:T(2,128)(2,1)S(1)} %all-to-all-done.rows_ref, ...), custom_call_target="tpu_custom_call" | custom-call | tf_op jit(solution)/shard_map/pallas_call | solution.py:33
  56.7 4.7 %collective-permute-start.3 = (bf16[1152,384]{1,0:T(8,128)(2,1)}, bf16[1152,384]{1,0:T(8,128)(2,1)S(1)}, u32[]{:S(2)}, u32[]{:S(2)}) collective-permute-start(bf16[1152,384]{1,0:T(8,128)(2,1)} %get-tuple-element.23), channel_id=1, source_target_pairs={{0,256},{128,384},{256,0},{384,128},{1,257},{129,385},{257,1},{385... | collective-permute-start | bytes 2654216 | tf_op jit(solution)/shard_map/ppermute | solution.py:210
  61.4 13.7 %all-to-all-start.1 = ((bf16[128,2,1664]{2,1,0:T(2,128)(2,1)}), bf16[128,2,1664]{2,1,0:T(2,128)(2,1)S(1)}, u32[]{:S(2)}, u32[]{:S(2)}) async-start(bf16[128,2,1664]{2,1,0:T(2,128)(2,1)} %get-tuple-element.19), calls=%async_computation.1 | async-start | bytes 1703936 | tf_op jit(solution)/shard_map/all_to_all | solution.py:271
  75.2 3.3 %collective-permute-start.4 = (bf16[1152,384]{1,0:T(8,128)(2,1)}, bf16[1152,384]{1,0:T(8,128)(2,1)S(1)}, u32[]{:S(2)}, u32[]{:S(2)}) collective-permute-start(bf16[1152,384]{1,0:T(8,128)(2,1)} %get-tuple-element.24), channel_id=1, source_target_pairs={{0,128},{128,256},{256,384},{384,0},{1,129},{129,257},{257,385},{3... | collective-permute-start | bytes 2654216 | tf_op jit(solution)/shard_map/ppermute | solution.py:210
  78.5 2.5 %collective-permute-start.5 = (bf16[1152,384]{1,0:T(8,128)(2,1)}, bf16[1152,384]{1,0:T(8,128)(2,1)S(1)}, u32[]{:S(2)}, u32[]{:S(2)}) collective-permute-start(bf16[1152,384]{1,0:T(8,128)(2,1)} %get-tuple-element.25), channel_id=1, source_target_pairs={{0,384},{128,0},{256,128},{384,256},{1,385},{129,1},{257,129},{385... | collective-permute-start | bytes 2654216 | tf_op jit(solution)/shard_map/ppermute | solution.py:210
  81.1 1.2 %copy-done.3 = bf16[1152,384]{1,0:T(8,128)(2,1)S(1)} copy-done((bf16[1152,384]{1,0:T(8,128)(2,1)S(1)}, bf16[1152,384]{1,0:T(8,128)(2,1)}, u32[]{:S(2)}) %copy-start.3) | copy-done | bytes 884760
  82.2 0.9 shard_map.114.sum_ref
  83.1 0.0 copy-start.1
  83.2 0.0 copy-start.2
  83.2 17.7 %collective-permute-done.4.a_ref = bf16[1152,384]{1,0:T(8,128)(2,1)S(1)} collective-permute-done((bf16[1152,384]{1,0:T(8,128)(2,1)}, bf16[1152,384]{1,0:T(8,128)(2,1)S(1)}, u32[]{:S(2)}, u32[]{:S(2)}) %collective-permute-start.4) | collective-permute-done | bytes 884768 | tf_op jit(solution)/shard_map/ppermute | solution.py:210
  100.9 2.4 %collective-permute-done.5.b_ref = bf16[1152,384]{1,0:T(8,128)(2,1)S(1)} collective-permute-done((bf16[1152,384]{1,0:T(8,128)(2,1)}, bf16[1152,384]{1,0:T(8,128)(2,1)S(1)}, u32[]{:S(2)}, u32[]{:S(2)}) %collective-permute-start.5) | collective-permute-done | bytes 884768 | tf_op jit(solution)/shard_map/ppermute | solution.py:210
  103.2 1.0 shard_map.115
  104.3 1.2 %shard_map.113 = (bf16[16,1536]{1,0:T(8,128)(2,1)}, f32[8,16]{1,0:T(8,128)}) custom-call(s32[8,16]{1,0:T(8,128)S(1)} %bitcast.13, f32[8,16]{1,0:T(8,128)S(1)} %bitcast.15, bf16[128,2,1664]{2,1,0:T(2,128)(2,1)S(1)} %all-to-all-done.1.back_ref), custom_call_target="tpu_custom_call" | custom-call | tf_op jit(solution)/shard_map/pallas_call | solution.py:33
  (8 shorter events, 0.0 us)
Async XLA Ops:
  3.6 27.8 %collective-permute-start = (bf16[1152,384]{1,0:T(8,128)(2,1)}, bf16[1152,384]{1,0:T(8,128)(2,1)S(1)}, u32[]{:S(2)}, u32[]{:S(2)}) collective-permute-start(bf16[1152,384]{1,0:T(8,128)(2,1)} %get-tuple-element.18.own), channel_id=1, source_target_pairs={{0,256},{128,384},{256,0},{384,128},{1,257},{129,385},{257,1},{385... | collective-permute-start | bytes 2654216 | tf_op jit(solution)/shard_map/ppermute | solution.py:210
  6.9 43.7 %all-to-all-start = ((bf16[128,2,1536]{2,1,0:T(2,128)(2,1)}), bf16[128,2,1536]{2,1,0:T(2,128)(2,1)S(1)}, u32[]{:S(2)}, u32[]{:S(2)}) async-start(bf16[128,2,1536]{2,1,0:T(2,128)(2,1)} %get-tuple-element.17), calls=%async_computation | async-start | bytes 1572864 | tf_op jit(solution)/shard_map/all_to_all | solution.py:239
  24.3 25.1 %collective-permute-start.2 = (bf16[1152,384]{1,0:T(8,128)(2,1)}, bf16[1152,384]{1,0:T(8,128)(2,1)}, u32[]{:S(2)}, u32[]{:S(2)}) collective-permute-start(bf16[1152,384]{1,0:T(8,128)(2,1)} %get-tuple-element.18.own), channel_id=1, source_target_pairs={{0,384},{128,0},{256,128},{384,256},{1,385},{129,1},{257,129},{385... | collective-permute-start | bytes 2654216 | tf_op jit(solution)/shard_map/ppermute | solution.py:210
  26.2 24.4 %collective-permute-start.1 = (bf16[1152,384]{1,0:T(8,128)(2,1)}, bf16[1152,384]{1,0:T(8,128)(2,1)}, u32[]{:S(2)}, u32[]{:S(2)}) collective-permute-start(bf16[1152,384]{1,0:T(8,128)(2,1)} %get-tuple-element.18.own), channel_id=1, source_target_pairs={{0,128},{128,256},{256,384},{384,0},{1,129},{129,257},{257,385},{3... | collective-permute-start | bytes 2654216 | tf_op jit(solution)/shard_map/ppermute | solution.py:210
  31.4 1.0 copy-start.4
  32.4 18.2 %copy-start = (bf16[1,1,256,1536]{3,2,1,0:T(8,128)(2,1)S(1)}, bf16[1,1,256,1536]{3,2,1,0:T(8,128)(2,1)}, u32[]{:S(2)}) copy-start(bf16[1,1,256,1536]{3,2,1,0:T(8,128)(2,1)} %param.10) | copy-start | bytes 2359300
  56.7 24.3 %collective-permute-start.3 = (bf16[1152,384]{1,0:T(8,128)(2,1)}, bf16[1152,384]{1,0:T(8,128)(2,1)S(1)}, u32[]{:S(2)}, u32[]{:S(2)}) collective-permute-start(bf16[1152,384]{1,0:T(8,128)(2,1)} %get-tuple-element.23), channel_id=1, source_target_pairs={{0,256},{128,384},{256,0},{384,128},{1,257},{129,385},{257,1},{385... | collective-permute-start | bytes 2654216 | tf_op jit(solution)/shard_map/ppermute | solution.py:210
  61.4 42.8 %all-to-all-start.1 = ((bf16[128,2,1664]{2,1,0:T(2,128)(2,1)}), bf16[128,2,1664]{2,1,0:T(2,128)(2,1)S(1)}, u32[]{:S(2)}, u32[]{:S(2)}) async-start(bf16[128,2,1664]{2,1,0:T(2,128)(2,1)} %get-tuple-element.19), calls=%async_computation.1 | async-start | bytes 1703936 | tf_op jit(solution)/shard_map/all_to_all | solution.py:271
  75.2 25.7 %collective-permute-start.4 = (bf16[1152,384]{1,0:T(8,128)(2,1)}, bf16[1152,384]{1,0:T(8,128)(2,1)S(1)}, u32[]{:S(2)}, u32[]{:S(2)}) collective-permute-start(bf16[1152,384]{1,0:T(8,128)(2,1)} %get-tuple-element.24), channel_id=1, source_target_pairs={{0,128},{128,256},{256,384},{384,0},{1,129},{129,257},{257,385},{3... | collective-permute-start | bytes 2654216 | tf_op jit(solution)/shard_map/ppermute | solution.py:210
  78.5 24.7 %collective-permute-start.5 = (bf16[1152,384]{1,0:T(8,128)(2,1)}, bf16[1152,384]{1,0:T(8,128)(2,1)S(1)}, u32[]{:S(2)}, u32[]{:S(2)}) collective-permute-start(bf16[1152,384]{1,0:T(8,128)(2,1)} %get-tuple-element.25), channel_id=1, source_target_pairs={{0,384},{128,0},{256,128},{384,256},{1,385},{129,1},{257,129},{385... | collective-permute-start | bytes 2654216 | tf_op jit(solution)/shard_map/ppermute | solution.py:210
  81.0 1.2 %copy-start.3 = (bf16[1152,384]{1,0:T(8,128)(2,1)S(1)}, bf16[1152,384]{1,0:T(8,128)(2,1)}, u32[]{:S(2)}) copy-start(bf16[1152,384]{1,0:T(8,128)(2,1)} %get-tuple-element.22.own) | copy-start | bytes 2654212
  83.1 21.1 %copy-start.1 = (s32[16,8]{0,1:T(8,128)S(1)}, s32[16,8]{0,1:T(8,128)}, u32[]{:S(2)}) copy-start(s32[16,8]{0,1:T(8,128)} %param.8) | copy-start | bytes 1540
  83.2 21.1 %copy-start.2 = (f32[16,8]{0,1:T(8,128)S(1)}, f32[16,8]{0,1:T(8,128)}, u32[]{:S(2)}) copy-start(f32[16,8]{0,1:T(8,128)} %param.9) | copy-start | bytes 1540

commit v4 on v3

--- a/solution.py
+++ b/solution.py
@@ -9,9 +9,11 @@
 EXTRA = 128
 BF = jnp.bfloat16
 F32 = jnp.float32
-PRE_COST = 12000 << 20
+PRE_COST = 9000 << 20
 SUM_COST = 12000 << 20
-MID_MIB = 52
+MID_MIB = 50
+EARLY_MIB = 50
+EARLY_COST = 3000 << 20
 LAST_MIB = 20
 
 
@@ -134,31 +136,43 @@
     finish(start([(acc_ref, acc_hbm)], sems))
 
 
+def early_kernel(
+    x_ref, rows_ref, acc_hbm, own, right, far, acc_out, dh_ref, g_ref, acc_ref, w_ref, wd_ref, sems
+):
+    slots, n, f = x_ref.shape[0], x_ref.shape[1] // 4, dh_ref.shape[1]
+    blocks = ((3, right), (0, own), (2, far))
+    moves = [(b.at[pl.ds(2 * n, n), :], wd_ref.at[k]) for k, (_, b) in enumerate(blocks)]
+    moves += [(right.at[pl.ds(k * n, n), :], w_ref.at[:, pl.ds(k * f, f)]) for k in (0, 1)]
+    moves += [(acc_hbm, acc_ref)]
+    copies = start(moves, sems)
+    for i in range(4):
+        cols = slice(i * n, (i + 1) * n)
+        g_ref[:, cols] = rows_ref[:, :, cols].reshape(slots, n)
+    finish(copies[0:3])
+    dh = None
+    for k, (offset, _) in enumerate(blocks):
+        term = dot(g_ref[:, span(offset, n)], wd_ref[k])
+        dh = term if dh is None else dh + term
+    dh_ref[...] = dh
+    finish(copies[3:])
+    acc_out[...] = acc_ref[...] + dot(x_ref[:, span(3, n)], w_ref[...])
+
+
 def middle_kernel(
-    x_ref, rows_ref, acc_hbm, own, right, left, far,
+    x_ref, g_ref, acc_ref, dh_ref, own, right, left, far,
     back_hbm, to_own, to_right, to_left, to_far,
-    acc_ref, w_ref, wd_ref, g_ref, back_ref, part_ref, sems,
+    w_ref, wd_ref, back_ref, part_ref, sems,
 ):
     width, n, f = x_ref.shape[1], x_ref.shape[1] // 4, wd_ref.shape[1]
-    blocks = ((3, right), (1, left), (0, own), (2, far))
-    moves = [(b.at[pl.ds(2 * n, n), :], wd_ref.at[span(i, n), :]) for i, b in blocks]
-    moves += [(acc_hbm, acc_ref)]
-    for i, b in blocks:
+    slots, shape = x_ref.shape[0], back_ref.shape
+    moves = [(left.at[pl.ds(2 * n, n), :], wd_ref)]
+    for i, b in ((1, left), (3, right), (0, own), (2, far)):
         moves += [(b.at[pl.ds(k * n, n), :], w_ref.at[span(i, n), pl.ds(k * f, f)]) for k in (0, 1)]
     copies = start(moves, sems)
-    slots, shape = x_ref.shape[0], rows_ref.shape
-    finish(copies[0:4])
-    dh = None
-    for i in range(4):
-        cols = slice(i * n, (i + 1) * n)
-        rows = rows_ref[:, :, cols].reshape(slots, n)
-        g_ref[:, cols] = rows
-        term = dot(rows, wd_ref[cols, :])
-        dh = term if dh is None else dh + term
-    finish(copies[4:9])
-    pre = acc_ref[...]
-    for offset in (3, 1):
-        pre = pre + dot(x_ref[:, span(offset, n)], w_ref[span(offset, n), :])
+    last = span(1, n)
+    finish(copies[0:3])
+    dh = dh_ref[...] + dot(g_ref[:, last], wd_ref[...])
+    pre = acc_ref[...] + dot(x_ref[:, last], w_ref[last, :])
     gate, up = pre[:, :f], pre[:, f:]
     sig = jax.nn.sigmoid(gate)
     act = gate * sig
@@ -176,7 +190,7 @@
         part_ref[k, n : 2 * n, :] = part[:, f:]
         part_ref[k, 2 * n :, :] = dot_tn(g_ref[:, cols], hidden).astype(BF)
         out += start([(part_ref.at[k], to)], sems.at[pl.ds(15 + k, 1)])
-    finish(copies[9:13])
+    finish(copies[3:9])
     for i in range(4):
         at = slice(i * n, (i + 1) * n)
         back_ref[:, :, at] = dot_nt(both, w_ref[at, :]).astype(BF).reshape(*shape[:2], n)
@@ -237,8 +251,8 @@
     )
     far = shift(own, 2)
     rows = lax.all_to_all(send, "expert", split_axis=0, concat_axis=0, tiled=True)
+    left = shift(own, -1)
     right = shift(own, 1)
-    left = shift(own, -1)
     (acc,) = call(
         pre_kernel,
         [((slots, 2 * f), F32)],
@@ -251,20 +265,32 @@
         ],
         flops=PRE_COST,
     )
+    acc, dh, g = call(
+        early_kernel,
+        [((slots, 2 * f), F32), ((slots, f), F32), ((slots, width), BF)],
+        (x, rows, acc, own, right, far),
+        [
+            pltpu.VMEM((slots, 2 * f), F32),
+            pltpu.VMEM((n, 2 * f), BF),
+            pltpu.VMEM((3, n, f), BF),
+            dma((6,)),
+        ],
+        flops=EARLY_COST,
+        where=(pltpu.VMEM,) * 2 + (pltpu.HBM,) * 4 + (pltpu.VMEM,) * 3,
+        mib=EARLY_MIB,
+    )
     row_grad, to_own, to_right, to_left, to_far = call(
         middle_kernel,
         [(row_block, BF)] + [block] * 4,
-        (x, rows, acc, own, right, left, far),
+        (x, g, acc, dh, own, right, left, far),
         [
-            pltpu.VMEM((slots, 2 * f), F32),
             pltpu.VMEM((width, 2 * f), BF),
-            pltpu.VMEM((width, f), BF),
-            pltpu.VMEM((slots, width), BF),
+            pltpu.VMEM((n, f), BF),
             pltpu.VMEM(row_block, BF),
             pltpu.VMEM((4, 3 * n, f), BF),
             dma((20,)),
         ],
-        where=(pltpu.VMEM,) * 2 + (pltpu.HBM,) * 10,
+        where=(pltpu.VMEM,) * 4 + (pltpu.HBM,) * 9,
         mib=MID_MIB,
     )
     from_far = shift(to_far, 2)

time: 106 us -> 107 us (level)
  waiting for transfers between devices: 35.3 us -> 37.5 us
  starting transfers between devices: 52 us -> 50 us
  Pallas kernels: 15.2 us -> 16.3 us
    ppermute x6, starting transfers between devices: 20.9 us -> 18.4 us  [shift(): return lax.ppermute(value, 'dp', [(i, (i + by) % 4) for i in range(4)])]
    all_to_all x1, waiting for transfers between devices: 0.01 us -> 1.95 us  [shards(): lax.all_to_all(send, 'expert', split_axis=0, concat_axis=0, tiled=True)]
    pallas_call x6 -> x7, Pallas kernels: 15.2 us -> 16.3 us  [call(): pl.pallas_call(body, out_shape=[jax.ShapeDtypeStruct(s, d) for s, d in ou...]
  transfers between devices with their start and end apart: 8 -> 8, of which waited for: 4 -> 6; matrix products, arithmetic and copies ran while one was open for 0% -> 0% of each run, Pallas kernels for 5% -> 7%
where the time goes in v4:
time: 107 us
  starting transfers between devices  50 us (47%)
  waiting for transfers between devices  37.5 us (35%)
  Pallas kernels  16.3 us (15%)
  local copies, waits for them, and re-layouts  2.16 us (2%)
    ppermute x6, waiting for transfers between devices, shift(): return lax.ppermute(value, 'dp', [(i, (i + by) % 4) for i in range(4)])  35.6 us
    ppermute x6, starting transfers between devices, shift(): return lax.ppermute(value, 'dp', [(i, (i + by) % 4) for i in range(4)])  18.4 us
    all_to_all x1, starting transfers between devices, shards(): lax.all_to_all(send, 'expert', split_axis=0, concat_axis=0, tiled=True)  17.4 us
    pallas_call x7, Pallas kernels, call(): pl.pallas_call(body, out_shape=[jax.ShapeDtypeStruct(s, d) for s, d in ou...  16.3 us
    all_to_all x1, starting transfers between devices, shards(): lax.all_to_all(row_grad, 'expert', split_axis=0, concat_axis=0, tiled=True)  14.2 us
    unnamed x10, local copies, waits for them, and re-layouts  2.16 us
  transfers between devices with their start and end apart: 8, of which 6 were waited for; matrix products, arithmetic and copies ran while one was open for 0% of the time, Pallas kernels for 7%

profile of v4, /device:TPU:14, one launch (start us, length us, event | category | flops | bytes accessed | tf_op | source)
XLA Modules:
  0.0 106.7 jit_solution(14075341443286847209)
XLA Ops:
  0.6 2.9 %shard_map.110 = (bf16[1152,384]{1,0:T(8,128)(2,1)}, bf16[128,2,1536]{2,1,0:T(2,128)(2,1)}) custom-call(bf16[384,384]{1,0:T(8,128)(2,1)} %bitcast.17, bf16[384,384]{1,0:T(8,128)(2,1)} %bitcast.18, bf16[384,384]{1,0:T(8,128)(2,1)} %bitcast.19, s32[8,16]{1,0:T(8,128)} %bitcast.13, f32[8,16]{1,0:T(8,128)} %bitcast.15, bf16[16,1536]{1,0:T(8,128)(2,1)} %grad_hbm.1), custom_call_target="tpu_custom_call" | custom-call | tf_op jit(solution)/shard_map/pallas_call | solution.py:35
  3.6 3.3 %collective-permute-start = (bf16[1152,384]{1,0:T(8,128)(2,1)}, bf16[1152,384]{1,0:T(8,128)(2,1)S(1)}, u32[]{:S(2)}, u32[]{:S(2)}) collective-permute-start(bf16[1152,384]{1,0:T(8,128)(2,1)} %get-tuple-element.21.own), channel_id=1, source_target_pairs={{0,256},{128,384},{256,0},{384,128},{1,257},{129,385},{257,1},{385... | collective-permute-start | bytes 2654216 | tf_op jit(solution)/shard_map/ppermute | solution.py:224
  6.9 17.4 %all-to-all-start = ((bf16[128,2,1536]{2,1,0:T(2,128)(2,1)}), bf16[128,2,1536]{2,1,0:T(2,128)(2,1)S(1)}, u32[]{:S(2)}, u32[]{:S(2)}) async-start(bf16[128,2,1536]{2,1,0:T(2,128)(2,1)} %get-tuple-element.20), calls=%async_computation | async-start | bytes 1572864 | tf_op jit(solution)/shard_map/all_to_all | solution.py:253
  24.3 4.0 %collective-permute-start.1 = (bf16[1152,384]{1,0:T(8,128)(2,1)}, bf16[1152,384]{1,0:T(8,128)(2,1)}, u32[]{:S(2)}, u32[]{:S(2)}) collective-permute-start(bf16[1152,384]{1,0:T(8,128)(2,1)} %get-tuple-element.21.own), channel_id=1, source_target_pairs={{0,128},{128,256},{256,384},{384,0},{1,129},{129,257},{257,385},{3... | collective-permute-start | bytes 2654216 | tf_op jit(solution)/shard_map/ppermute | solution.py:224
  28.3 1.9 %collective-permute-start.2 = (bf16[1152,384]{1,0:T(8,128)(2,1)}, bf16[1152,384]{1,0:T(8,128)(2,1)}, u32[]{:S(2)}, u32[]{:S(2)}) collective-permute-start(bf16[1152,384]{1,0:T(8,128)(2,1)} %get-tuple-element.21.own), channel_id=1, source_target_pairs={{0,384},{128,0},{256,128},{384,256},{1,385},{129,1},{257,129},{385... | collective-permute-start | bytes 2654216 | tf_op jit(solution)/shard_map/ppermute | solution.py:224
  30.2 1.0 copy-done.4
  31.2 2.9 %shard_map.111.acc_hbm = f32[256,768]{1,0:T(8,128)} custom-call(bf16[256,1536]{1,0:T(8,128)(2,1)} %bitcast.10, bf16[1152,384]{1,0:T(8,128)(2,1)} %get-tuple-element.21.own, bf16[1152,384]{1,0:T(8,128)(2,1)} %copy-done.4), custom_call_target="tpu_custom_call" | custom-call | flops 9437184000 | tf_op jit(solution)/shard_map/pallas_call | solution.py:35
  34.1 14.1 %collective-permute-done.1.right = bf16[1152,384]{1,0:T(8,128)(2,1)} collective-permute-done((bf16[1152,384]{1,0:T(8,128)(2,1)}, bf16[1152,384]{1,0:T(8,128)(2,1)}, u32[]{:S(2)}, u32[]{:S(2)}) %collective-permute-start.1) | collective-permute-done | bytes 884768 | tf_op jit(solution)/shard_map/ppermute | solution.py:224
  48.2 1.9 %all-to-all-done.rows_ref = bf16[128,2,1536]{2,1,0:T(2,128)(2,1)S(1)} async-done(((bf16[128,2,1536]{2,1,0:T(2,128)(2,1)}), bf16[128,2,1536]{2,1,0:T(2,128)(2,1)S(1)}, u32[]{:S(2)}, u32[]{:S(2)}) %all-to-all-start) | async-done | bytes 786464 | tf_op jit(solution)/shard_map/all_to_all | solution.py:253
  50.1 2.2 %shard_map.112 = (f32[256,768]{1,0:T(8,128)S(1)}, f32[256,384]{1,0:T(8,128)S(1)}, bf16[256,1536]{1,0:T(8,128)(2,1)S(1)}) custom-call(bf16[256,1536]{1,0:T(8,128)(2,1)S(1)} %bitcast.11, bf16[128,2,1536]{2,1,0:T(2,128)(2,1)S(1)} %all-to-all-done.rows_ref, f32[256,768]{1,0:T(8,128)} %shard_map.111.acc_hbm, bf16[1152,384]{1,0:T(8,128)(2,1)} %get-tuple-element.21.own, ...), custom_call_target="tpu_custom_call" | custom-call | flops 3145728000 | tf_op jit(solution)/shard_map/pallas_call | solution.py:35
  52.3 0.8 collective-permute-done.2.left
  53.1 5.1 %shard_map.113 = (bf16[128,2,1664]{2,1,0:T(2,128)(2,1)}, bf16[1152,384]{1,0:T(8,128)(2,1)}, bf16[1152,384]{1,0:T(8,128)(2,1)}, bf16[1152,384]{1,0:T(8,128)(2,1)}, bf16[1152,384]{1,0:T(8,128)(2,1)}) custom-call(bf16[256,1536]{1,0:T(8,128)(2,1)S(1)} %bitcast.12, bf16[256,1536]{1,0:T(8,128)(2,1)S(1)} %get-tuple-element.22.g_ref, ...), custom_call_target="tpu_custom_call" | custom-call | tf_op jit(solution)/shard_map/pallas_call | solution.py:35
  58.2 3.3 %collective-permute-start.3 = (bf16[1152,384]{1,0:T(8,128)(2,1)}, bf16[1152,384]{1,0:T(8,128)(2,1)S(1)}, u32[]{:S(2)}, u32[]{:S(2)}) collective-permute-start(bf16[1152,384]{1,0:T(8,128)(2,1)} %get-tuple-element.29), channel_id=1, source_target_pairs={{0,256},{128,384},{256,0},{384,128},{1,257},{129,385},{257,1},{385... | collective-permute-start | bytes 2654216 | tf_op jit(solution)/shard_map/ppermute | solution.py:224
  61.5 14.2 %all-to-all-start.1 = ((bf16[128,2,1664]{2,1,0:T(2,128)(2,1)}), bf16[128,2,1664]{2,1,0:T(2,128)(2,1)S(1)}, u32[]{:S(2)}, u32[]{:S(2)}) async-start(bf16[128,2,1664]{2,1,0:T(2,128)(2,1)} %get-tuple-element.25), calls=%async_computation.1 | async-start | bytes 1703936 | tf_op jit(solution)/shard_map/all_to_all | solution.py:297
  75.7 3.9 %collective-permute-start.4 = (bf16[1152,384]{1,0:T(8,128)(2,1)}, bf16[1152,384]{1,0:T(8,128)(2,1)S(1)}, u32[]{:S(2)}, u32[]{:S(2)}) collective-permute-start(bf16[1152,384]{1,0:T(8,128)(2,1)} %get-tuple-element.30), channel_id=1, source_target_pairs={{0,128},{128,256},{256,384},{384,0},{1,129},{129,257},{257,385},{3... | collective-permute-start | bytes 2654216 | tf_op jit(solution)/shard_map/ppermute | solution.py:224
  79.7 1.9 %collective-permute-start.5 = (bf16[1152,384]{1,0:T(8,128)(2,1)}, bf16[1152,384]{1,0:T(8,128)(2,1)S(1)}, u32[]{:S(2)}, u32[]{:S(2)}) collective-permute-start(bf16[1152,384]{1,0:T(8,128)(2,1)} %get-tuple-element.31), channel_id=1, source_target_pairs={{0,384},{128,0},{256,128},{384,256},{1,385},{129,1},{257,129},{385... | collective-permute-start | bytes 2654216 | tf_op jit(solution)/shard_map/ppermute | solution.py:224
  81.6 0.8 collective-permute-done.3.far
  82.4 1.2 %copy-done.3 = bf16[1152,384]{1,0:T(8,128)(2,1)S(1)} copy-done((bf16[1152,384]{1,0:T(8,128)(2,1)S(1)}, bf16[1152,384]{1,0:T(8,128)(2,1)}, u32[]{:S(2)}) %copy-start.3) | copy-done | bytes 884760
  83.5 0.9 shard_map.115.sum_ref
  84.5 0.0 copy-start.1
  84.5 15.1 %collective-permute-done.4.a_ref = bf16[1152,384]{1,0:T(8,128)(2,1)S(1)} collective-permute-done((bf16[1152,384]{1,0:T(8,128)(2,1)}, bf16[1152,384]{1,0:T(8,128)(2,1)S(1)}, u32[]{:S(2)}, u32[]{:S(2)}) %collective-permute-start.4) | collective-permute-done | bytes 884768 | tf_op jit(solution)/shard_map/ppermute | solution.py:224
  99.6 4.8 %collective-permute-done.5.b_ref = bf16[1152,384]{1,0:T(8,128)(2,1)S(1)} collective-permute-done((bf16[1152,384]{1,0:T(8,128)(2,1)}, bf16[1152,384]{1,0:T(8,128)(2,1)S(1)}, u32[]{:S(2)}, u32[]{:S(2)}) %collective-permute-start.5) | collective-permute-done | bytes 884768 | tf_op jit(solution)/shard_map/ppermute | solution.py:224
  104.4 1.0 shard_map.116
  105.5 1.2 %shard_map.114 = (bf16[16,1536]{1,0:T(8,128)(2,1)}, f32[8,16]{1,0:T(8,128)}) custom-call(s32[8,16]{1,0:T(8,128)S(1)} %bitcast.14, f32[8,16]{1,0:T(8,128)S(1)} %bitcast.16, bf16[128,2,1664]{2,1,0:T(2,128)(2,1)S(1)} %all-to-all-done.1.back_ref), custom_call_target="tpu_custom_call" | custom-call | tf_op jit(solution)/shard_map/pallas_call | solution.py:35
  (9 shorter events, 0.0 us)
Async XLA Ops:
  3.6 26.7 %collective-permute-start = (bf16[1152,384]{1,0:T(8,128)(2,1)}, bf16[1152,384]{1,0:T(8,128)(2,1)S(1)}, u32[]{:S(2)}, u32[]{:S(2)}) collective-permute-start(bf16[1152,384]{1,0:T(8,128)(2,1)} %get-tuple-element.21.own), channel_id=1, source_target_pairs={{0,256},{128,384},{256,0},{384,128},{1,257},{129,385},{257,1},{385... | collective-permute-start | bytes 2654216 | tf_op jit(solution)/shard_map/ppermute | solution.py:224
  6.9 43.3 %all-to-all-start = ((bf16[128,2,1536]{2,1,0:T(2,128)(2,1)}), bf16[128,2,1536]{2,1,0:T(2,128)(2,1)S(1)}, u32[]{:S(2)}, u32[]{:S(2)}) async-start(bf16[128,2,1536]{2,1,0:T(2,128)(2,1)} %get-tuple-element.20), calls=%async_computation | async-start | bytes 1572864 | tf_op jit(solution)/shard_map/all_to_all | solution.py:253
  24.3 23.9 %collective-permute-start.1 = (bf16[1152,384]{1,0:T(8,128)(2,1)}, bf16[1152,384]{1,0:T(8,128)(2,1)}, u32[]{:S(2)}, u32[]{:S(2)}) collective-permute-start(bf16[1152,384]{1,0:T(8,128)(2,1)} %get-tuple-element.21.own), channel_id=1, source_target_pairs={{0,128},{128,256},{256,384},{384,0},{1,129},{129,257},{257,385},{3... | collective-permute-start | bytes 2654216 | tf_op jit(solution)/shard_map/ppermute | solution.py:224
  28.3 24.8 %collective-permute-start.2 = (bf16[1152,384]{1,0:T(8,128)(2,1)}, bf16[1152,384]{1,0:T(8,128)(2,1)}, u32[]{:S(2)}, u32[]{:S(2)}) collective-permute-start(bf16[1152,384]{1,0:T(8,128)(2,1)} %get-tuple-element.21.own), channel_id=1, source_target_pairs={{0,384},{128,0},{256,128},{384,256},{1,385},{129,1},{257,129},{385... | collective-permute-start | bytes 2654216 | tf_op jit(solution)/shard_map/ppermute | solution.py:224
  30.2 1.0 copy-start.4
  31.2 18.9 %copy-start = (bf16[1,1,256,1536]{3,2,1,0:T(8,128)(2,1)S(1)}, bf16[1,1,256,1536]{3,2,1,0:T(8,128)(2,1)}, u32[]{:S(2)}) copy-start(bf16[1,1,256,1536]{3,2,1,0:T(8,128)(2,1)} %param.10) | copy-start | bytes 2359300
  58.2 24.2 %collective-permute-start.3 = (bf16[1152,384]{1,0:T(8,128)(2,1)}, bf16[1152,384]{1,0:T(8,128)(2,1)S(1)}, u32[]{:S(2)}, u32[]{:S(2)}) collective-permute-start(bf16[1152,384]{1,0:T(8,128)(2,1)} %get-tuple-element.29), channel_id=1, source_target_pairs={{0,256},{128,384},{256,0},{384,128},{1,257},{129,385},{257,1},{385... | collective-permute-start | bytes 2654216 | tf_op jit(solution)/shard_map/ppermute | solution.py:224
  61.5 44.0 %all-to-all-start.1 = ((bf16[128,2,1664]{2,1,0:T(2,128)(2,1)}), bf16[128,2,1664]{2,1,0:T(2,128)(2,1)S(1)}, u32[]{:S(2)}, u32[]{:S(2)}) async-start(bf16[128,2,1664]{2,1,0:T(2,128)(2,1)} %get-tuple-element.25), calls=%async_computation.1 | async-start | bytes 1703936 | tf_op jit(solution)/shard_map/all_to_all | solution.py:297
  75.7 23.9 %collective-permute-start.4 = (bf16[1152,384]{1,0:T(8,128)(2,1)}, bf16[1152,384]{1,0:T(8,128)(2,1)S(1)}, u32[]{:S(2)}, u32[]{:S(2)}) collective-permute-start(bf16[1152,384]{1,0:T(8,128)(2,1)} %get-tuple-element.30), channel_id=1, source_target_pairs={{0,128},{128,256},{256,384},{384,0},{1,129},{129,257},{257,385},{3... | collective-permute-start | bytes 2654216 | tf_op jit(solution)/shard_map/ppermute | solution.py:224
  79.7 24.7 %collective-permute-start.5 = (bf16[1152,384]{1,0:T(8,128)(2,1)}, bf16[1152,384]{1,0:T(8,128)(2,1)S(1)}, u32[]{:S(2)}, u32[]{:S(2)}) collective-permute-start(bf16[1152,384]{1,0:T(8,128)(2,1)} %get-tuple-element.31), channel_id=1, source_target_pairs={{0,384},{128,0},{256,128},{384,256},{1,385},{129,1},{257,129},{385... | collective-permute-start | bytes 2654216 | tf_op jit(solution)/shard_map/ppermute | solution.py:224
  82.4 1.2 %copy-start.3 = (bf16[1152,384]{1,0:T(8,128)(2,1)S(1)}, bf16[1152,384]{1,0:T(8,128)(2,1)}, u32[]{:S(2)}) copy-start(bf16[1152,384]{1,0:T(8,128)(2,1)} %get-tuple-element.28.own) | copy-start | bytes 2654212
  84.5 21.0 %copy-start.1 = (s32[16,8]{0,1:T(8,128)S(1)}, s32[16,8]{0,1:T(8,128)}, u32[]{:S(2)}) copy-start(s32[16,8]{0,1:T(8,128)} %param.8) | copy-start | bytes 1540
  84.5 21.0 %copy-start.2 = (f32[16,8]{0,1:T(8,128)S(1)}, f32[16,8]{0,1:T(8,128)}, u32[]{:S(2)}) copy-start(f32[16,8]{0,1:T(8,128)} %param.9) | copy-start | bytes 1540

commit v5 on v3

--- a/solution.py
+++ b/solution.py
@@ -147,14 +147,11 @@
         moves += [(b.at[pl.ds(k * n, n), :], w_ref.at[span(i, n), pl.ds(k * f, f)]) for k in (0, 1)]
     copies = start(moves, sems)
     slots, shape = x_ref.shape[0], rows_ref.shape
-    finish(copies[0:4])
-    dh = None
     for i in range(4):
         cols = slice(i * n, (i + 1) * n)
-        rows = rows_ref[:, :, cols].reshape(slots, n)
-        g_ref[:, cols] = rows
-        term = dot(rows, wd_ref[cols, :])
-        dh = term if dh is None else dh + term
+        g_ref[:, cols] = rows_ref[:, :, cols].reshape(slots, n)
+    finish(copies[0:4])
+    dh = dot(g_ref[...], wd_ref[...])
     finish(copies[4:9])
     pre = acc_ref[...]
     for offset in (3, 1):

time: 106 us -> 106 us (level)
  no operation moved by 1% of the time
where the time goes in v5:
time: 106 us
  starting transfers between devices  52 us (49%)
  waiting for transfers between devices  35.3 us (33%)
  Pallas kernels  15.2 us (14%)
  local copies, waits for them, and re-layouts  2.16 us (2%)
    ppermute x6, waiting for transfers between devices, shift(): return lax.ppermute(value, 'dp', [(i, (i + by) % 4) for i in range(4)])  35.3 us
    ppermute x6, starting transfers between devices, shift(): return lax.ppermute(value, 'dp', [(i, (i + by) % 4) for i in range(4)])  20.9 us
    all_to_all x1, starting transfers between devices, shards(): lax.all_to_all(send, 'expert', split_axis=0, concat_axis=0, tiled=True)  17.4 us
    pallas_call x6, Pallas kernels, call(): pl.pallas_call(body, out_shape=[jax.ShapeDtypeStruct(s, d) for s, d in ou...  15.2 us
    all_to_all x1, starting transfers between devices, shards(): lax.all_to_all(row_grad, 'expert', split_axis=0, concat_axis=0, tiled=True)  13.7 us
    unnamed x10, local copies, waits for them, and re-layouts  2.16 us
  transfers between devices with their start and end apart: 8, of which 4 were waited for; matrix products, arithmetic and copies ran while one was open for 0% of the time, Pallas kernels for 5%

profile of v5, /device:TPU:14, one launch (start us, length us, event | category | flops | bytes accessed | tf_op | source)
XLA Modules:
  0.0 105.5 jit_solution(16206459156058879541)
XLA Ops:
  0.6 2.9 %shard_map.110 = (bf16[1152,384]{1,0:T(8,128)(2,1)}, bf16[128,2,1536]{2,1,0:T(2,128)(2,1)}) custom-call(bf16[384,384]{1,0:T(8,128)(2,1)} %bitcast.16, bf16[384,384]{1,0:T(8,128)(2,1)} %bitcast.17, bf16[384,384]{1,0:T(8,128)(2,1)} %bitcast.18, s32[8,16]{1,0:T(8,128)} %bitcast.12, f32[8,16]{1,0:T(8,128)} %bitcast.14, bf16[16,1536]{1,0:T(8,128)(2,1)} %grad_hbm.1), custom_call_target="tpu_custom_call" | custom-call | tf_op jit(solution)/shard_map/pallas_call | solution.py:33
  3.6 3.3 %collective-permute-start = (bf16[1152,384]{1,0:T(8,128)(2,1)}, bf16[1152,384]{1,0:T(8,128)(2,1)S(1)}, u32[]{:S(2)}, u32[]{:S(2)}) collective-permute-start(bf16[1152,384]{1,0:T(8,128)(2,1)} %get-tuple-element.18.own), channel_id=1, source_target_pairs={{0,256},{128,384},{256,0},{384,128},{1,257},{129,385},{257,1},{385... | collective-permute-start | bytes 2654216 | tf_op jit(solution)/shard_map/ppermute | solution.py:207
  6.9 17.4 %all-to-all-start = ((bf16[128,2,1536]{2,1,0:T(2,128)(2,1)}), bf16[128,2,1536]{2,1,0:T(2,128)(2,1)S(1)}, u32[]{:S(2)}, u32[]{:S(2)}) async-start(bf16[128,2,1536]{2,1,0:T(2,128)(2,1)} %get-tuple-element.17), calls=%async_computation | async-start | bytes 1572864 | tf_op jit(solution)/shard_map/all_to_all | solution.py:236
  24.3 1.9 %collective-permute-start.2 = (bf16[1152,384]{1,0:T(8,128)(2,1)}, bf16[1152,384]{1,0:T(8,128)(2,1)}, u32[]{:S(2)}, u32[]{:S(2)}) collective-permute-start(bf16[1152,384]{1,0:T(8,128)(2,1)} %get-tuple-element.18.own), channel_id=1, source_target_pairs={{0,384},{128,0},{256,128},{384,256},{1,385},{129,1},{257,129},{385... | collective-permute-start | bytes 2654216 | tf_op jit(solution)/shard_map/ppermute | solution.py:207
  26.2 5.1 %collective-permute-start.1 = (bf16[1152,384]{1,0:T(8,128)(2,1)}, bf16[1152,384]{1,0:T(8,128)(2,1)}, u32[]{:S(2)}, u32[]{:S(2)}) collective-permute-start(bf16[1152,384]{1,0:T(8,128)(2,1)} %get-tuple-element.18.own), channel_id=1, source_target_pairs={{0,128},{128,256},{256,384},{384,0},{1,129},{129,257},{257,385},{3... | collective-permute-start | bytes 2654216 | tf_op jit(solution)/shard_map/ppermute | solution.py:207
  31.4 0.0 collective-permute-done.far
  31.4 1.0 copy-done.4
  32.4 2.9 %shard_map.111.acc_hbm = f32[256,768]{1,0:T(8,128)} custom-call(bf16[256,1536]{1,0:T(8,128)(2,1)} %bitcast.10, bf16[1152,384]{1,0:T(8,128)(2,1)} %get-tuple-element.18.own, bf16[1152,384]{1,0:T(8,128)(2,1)} %copy-done.4), custom_call_target="tpu_custom_call" | custom-call | flops 12582912000 | tf_op jit(solution)/shard_map/pallas_call | solution.py:33
  35.3 14.1 %collective-permute-done.2.left = bf16[1152,384]{1,0:T(8,128)(2,1)} collective-permute-done((bf16[1152,384]{1,0:T(8,128)(2,1)}, bf16[1152,384]{1,0:T(8,128)(2,1)}, u32[]{:S(2)}, u32[]{:S(2)}) %collective-permute-start.2) | collective-permute-done | bytes 884768 | tf_op jit(solution)/shard_map/ppermute | solution.py:207
  49.4 1.2 %collective-permute-done.1.right = bf16[1152,384]{1,0:T(8,128)(2,1)} collective-permute-done((bf16[1152,384]{1,0:T(8,128)(2,1)}, bf16[1152,384]{1,0:T(8,128)(2,1)}, u32[]{:S(2)}, u32[]{:S(2)}) %collective-permute-start.1) | collective-permute-done | bytes 884768 | tf_op jit(solution)/shard_map/ppermute | solution.py:207
  50.6 0.0 all-to-all-done.rows_ref
  50.6 6.1 %shard_map.112 = (bf16[128,2,1664]{2,1,0:T(2,128)(2,1)}, bf16[1152,384]{1,0:T(8,128)(2,1)}, bf16[1152,384]{1,0:T(8,128)(2,1)}, bf16[1152,384]{1,0:T(8,128)(2,1)}, bf16[1152,384]{1,0:T(8,128)(2,1)}) custom-call(bf16[256,1536]{1,0:T(8,128)(2,1)S(1)} %bitcast.11, bf16[128,2,1536]{2,1,0:T(2,128)(2,1)S(1)} %all-to-all-done.rows_ref, ...), custom_call_target="tpu_custom_call" | custom-call | tf_op jit(solution)/shard_map/pallas_call | solution.py:33
  56.7 4.7 %collective-permute-start.3 = (bf16[1152,384]{1,0:T(8,128)(2,1)}, bf16[1152,384]{1,0:T(8,128)(2,1)S(1)}, u32[]{:S(2)}, u32[]{:S(2)}) collective-permute-start(bf16[1152,384]{1,0:T(8,128)(2,1)} %get-tuple-element.23), channel_id=1, source_target_pairs={{0,256},{128,384},{256,0},{384,128},{1,257},{129,385},{257,1},{385... | collective-permute-start | bytes 2654216 | tf_op jit(solution)/shard_map/ppermute | solution.py:207
  61.4 13.7 %all-to-all-start.1 = ((bf16[128,2,1664]{2,1,0:T(2,128)(2,1)}), bf16[128,2,1664]{2,1,0:T(2,128)(2,1)S(1)}, u32[]{:S(2)}, u32[]{:S(2)}) async-start(bf16[128,2,1664]{2,1,0:T(2,128)(2,1)} %get-tuple-element.19), calls=%async_computation.1 | async-start | bytes 1703936 | tf_op jit(solution)/shard_map/all_to_all | solution.py:268
  75.2 3.3 %collective-permute-start.4 = (bf16[1152,384]{1,0:T(8,128)(2,1)}, bf16[1152,384]{1,0:T(8,128)(2,1)S(1)}, u32[]{:S(2)}, u32[]{:S(2)}) collective-permute-start(bf16[1152,384]{1,0:T(8,128)(2,1)} %get-tuple-element.24), channel_id=1, source_target_pairs={{0,128},{128,256},{256,384},{384,0},{1,129},{129,257},{257,385},{3... | collective-permute-start | bytes 2654216 | tf_op jit(solution)/shard_map/ppermute | solution.py:207
  78.5 2.6 %collective-permute-start.5 = (bf16[1152,384]{1,0:T(8,128)(2,1)}, bf16[1152,384]{1,0:T(8,128)(2,1)S(1)}, u32[]{:S(2)}, u32[]{:S(2)}) collective-permute-start(bf16[1152,384]{1,0:T(8,128)(2,1)} %get-tuple-element.25), channel_id=1, source_target_pairs={{0,384},{128,0},{256,128},{384,256},{1,385},{129,1},{257,129},{385... | collective-permute-start | bytes 2654216 | tf_op jit(solution)/shard_map/ppermute | solution.py:207
  81.0 1.2 %copy-done.3 = bf16[1152,384]{1,0:T(8,128)(2,1)S(1)} copy-done((bf16[1152,384]{1,0:T(8,128)(2,1)S(1)}, bf16[1152,384]{1,0:T(8,128)(2,1)}, u32[]{:S(2)}) %copy-start.3) | copy-done | bytes 884760
  82.2 0.9 shard_map.114.sum_ref
  83.1 0.0 copy-start.1
  83.2 0.0 copy-start.2
  83.2 17.7 %collective-permute-done.4.a_ref = bf16[1152,384]{1,0:T(8,128)(2,1)S(1)} collective-permute-done((bf16[1152,384]{1,0:T(8,128)(2,1)}, bf16[1152,384]{1,0:T(8,128)(2,1)S(1)}, u32[]{:S(2)}, u32[]{:S(2)}) %collective-permute-start.4) | collective-permute-done | bytes 884768 | tf_op jit(solution)/shard_map/ppermute | solution.py:207
  100.8 2.4 %collective-permute-done.5.b_ref = bf16[1152,384]{1,0:T(8,128)(2,1)S(1)} collective-permute-done((bf16[1152,384]{1,0:T(8,128)(2,1)}, bf16[1152,384]{1,0:T(8,128)(2,1)S(1)}, u32[]{:S(2)}, u32[]{:S(2)}) %collective-permute-start.5) | collective-permute-done | bytes 884768 | tf_op jit(solution)/shard_map/ppermute | solution.py:207
  103.2 1.0 shard_map.115
  104.3 1.2 %shard_map.113 = (bf16[16,1536]{1,0:T(8,128)(2,1)}, f32[8,16]{1,0:T(8,128)}) custom-call(s32[8,16]{1,0:T(8,128)S(1)} %bitcast.13, f32[8,16]{1,0:T(8,128)S(1)} %bitcast.15, bf16[128,2,1664]{2,1,0:T(2,128)(2,1)S(1)} %all-to-all-done.1.back_ref), custom_call_target="tpu_custom_call" | custom-call | tf_op jit(solution)/shard_map/pallas_call | solution.py:33
  (8 shorter events, 0.0 us)
Async XLA Ops:
  3.6 27.8 %collective-permute-start = (bf16[1152,384]{1,0:T(8,128)(2,1)}, bf16[1152,384]{1,0:T(8,128)(2,1)S(1)}, u32[]{:S(2)}, u32[]{:S(2)}) collective-permute-start(bf16[1152,384]{1,0:T(8,128)(2,1)} %get-tuple-element.18.own), channel_id=1, source_target_pairs={{0,256},{128,384},{256,0},{384,128},{1,257},{129,385},{257,1},{385... | collective-permute-start | bytes 2654216 | tf_op jit(solution)/shard_map/ppermute | solution.py:207
  6.9 43.7 %all-to-all-start = ((bf16[128,2,1536]{2,1,0:T(2,128)(2,1)}), bf16[128,2,1536]{2,1,0:T(2,128)(2,1)S(1)}, u32[]{:S(2)}, u32[]{:S(2)}) async-start(bf16[128,2,1536]{2,1,0:T(2,128)(2,1)} %get-tuple-element.17), calls=%async_computation | async-start | bytes 1572864 | tf_op jit(solution)/shard_map/all_to_all | solution.py:236
  24.3 25.1 %collective-permute-start.2 = (bf16[1152,384]{1,0:T(8,128)(2,1)}, bf16[1152,384]{1,0:T(8,128)(2,1)}, u32[]{:S(2)}, u32[]{:S(2)}) collective-permute-start(bf16[1152,384]{1,0:T(8,128)(2,1)} %get-tuple-element.18.own), channel_id=1, source_target_pairs={{0,384},{128,0},{256,128},{384,256},{1,385},{129,1},{257,129},{385... | collective-permute-start | bytes 2654216 | tf_op jit(solution)/shard_map/ppermute | solution.py:207
  26.2 24.4 %collective-permute-start.1 = (bf16[1152,384]{1,0:T(8,128)(2,1)}, bf16[1152,384]{1,0:T(8,128)(2,1)}, u32[]{:S(2)}, u32[]{:S(2)}) collective-permute-start(bf16[1152,384]{1,0:T(8,128)(2,1)} %get-tuple-element.18.own), channel_id=1, source_target_pairs={{0,128},{128,256},{256,384},{384,0},{1,129},{129,257},{257,385},{3... | collective-permute-start | bytes 2654216 | tf_op jit(solution)/shard_map/ppermute | solution.py:207
  31.4 1.0 copy-start.4
  32.4 18.2 %copy-start = (bf16[1,1,256,1536]{3,2,1,0:T(8,128)(2,1)S(1)}, bf16[1,1,256,1536]{3,2,1,0:T(8,128)(2,1)}, u32[]{:S(2)}) copy-start(bf16[1,1,256,1536]{3,2,1,0:T(8,128)(2,1)} %param.10) | copy-start | bytes 2359300
  56.7 24.3 %collective-permute-start.3 = (bf16[1152,384]{1,0:T(8,128)(2,1)}, bf16[1152,384]{1,0:T(8,128)(2,1)S(1)}, u32[]{:S(2)}, u32[]{:S(2)}) collective-permute-start(bf16[1152,384]{1,0:T(8,128)(2,1)} %get-tuple-element.23), channel_id=1, source_target_pairs={{0,256},{128,384},{256,0},{384,128},{1,257},{129,385},{257,1},{385... | collective-permute-start | bytes 2654216 | tf_op jit(solution)/shard_map/ppermute | solution.py:207
  61.4 42.8 %all-to-all-start.1 = ((bf16[128,2,1664]{2,1,0:T(2,128)(2,1)}), bf16[128,2,1664]{2,1,0:T(2,128)(2,1)S(1)}, u32[]{:S(2)}, u32[]{:S(2)}) async-start(bf16[128,2,1664]{2,1,0:T(2,128)(2,1)} %get-tuple-element.19), calls=%async_computation.1 | async-start | bytes 1703936 | tf_op jit(solution)/shard_map/all_to_all | solution.py:268
  75.2 25.7 %collective-permute-start.4 = (bf16[1152,384]{1,0:T(8,128)(2,1)}, bf16[1152,384]{1,0:T(8,128)(2,1)S(1)}, u32[]{:S(2)}, u32[]{:S(2)}) collective-permute-start(bf16[1152,384]{1,0:T(8,128)(2,1)} %get-tuple-element.24), channel_id=1, source_target_pairs={{0,128},{128,256},{256,384},{384,0},{1,129},{129,257},{257,385},{3... | collective-permute-start | bytes 2654216 | tf_op jit(solution)/shard_map/ppermute | solution.py:207
  78.5 24.7 %collective-permute-start.5 = (bf16[1152,384]{1,0:T(8,128)(2,1)}, bf16[1152,384]{1,0:T(8,128)(2,1)S(1)}, u32[]{:S(2)}, u32[]{:S(2)}) collective-permute-start(bf16[1152,384]{1,0:T(8,128)(2,1)} %get-tuple-element.25), channel_id=1, source_target_pairs={{0,384},{128,0},{256,128},{384,256},{1,385},{129,1},{257,129},{385... | collective-permute-start | bytes 2654216 | tf_op jit(solution)/shard_map/ppermute | solution.py:207
  81.0 1.2 %copy-start.3 = (bf16[1152,384]{1,0:T(8,128)(2,1)S(1)}, bf16[1152,384]{1,0:T(8,128)(2,1)}, u32[]{:S(2)}) copy-start(bf16[1152,384]{1,0:T(8,128)(2,1)} %get-tuple-element.22.own) | copy-start | bytes 2654212
  83.1 21.1 %copy-start.1 = (s32[16,8]{0,1:T(8,128)S(1)}, s32[16,8]{0,1:T(8,128)}, u32[]{:S(2)}) copy-start(s32[16,8]{0,1:T(8,128)} %param.8) | copy-start | bytes 1540
  83.2 21.1 %copy-start.2 = (f32[16,8]{0,1:T(8,128)S(1)}, f32[16,8]{0,1:T(8,128)}, u32[]{:S(2)}) copy-start(f32[16,8]{0,1:T(8,128)} %param.9) | copy-start | bytes 1540
